TPU v7x, 256 devices: a whole 4x4x8 slice. The times are simulated.
256 devices in a mesh: section: 2 (over y_lo), row: 16 (over z, y_hi), col: 8 (over x, core).
Axes of the slice: x: 4, y: 4 (y_hi: 2, y_lo: 2; y = y_hi * 2 + y_lo), z: 8, core: 2. Of those that a mesh axis runs over, the one named last changes fastest.
Arguments:
- tokens: float32 [4, 1024, 3072], P(None, 'row', 'col'), may hold values from -30 to 30
- batch_order: int32 [4], replicated, may hold values from 0 to 3, each once
- modulation: float32 [4, 5, 3072], replicated, may hold values from -3 to 3
- expand_weight: bfloat16 [3072, 12288], P('row', 'col'), may hold values from -0.109375 to 0.109375
- expand_bias: float32 [12288], P('col'), may hold values from -3 to 3
- reduce_weight: bfloat16 [12288, 3072], P('col', 'row'), may hold values from -0.0546875 to 0.0546875
- reduce_bias: float32 [3072], P('col'), may hold values from -3 to 3
- patch_weight: float32 [3072, 64], P('col'), may hold values from -0.109375 to 0.109375
- patch_bias: float32 [64], replicated, may hold values from -3 to 3
- latent_kernel: float32 [3, 3, 16, 512], replicated, may hold values from -0.5 to 0.5
- latent_bias: float32 [512], replicated, may hold values from -4 to 4
- group_gain: float32 [512], replicated, may hold values from 0.1 to 1.9
- group_shift: float32 [512], replicated, may hold values from -3 to 3
- decode_kernel: bfloat16 [3, 3, 512, 512], P(None, None, None, 'section'), may hold values from -0.09375 to 0.09375
- decode_bias: float32 [512], P('section'), may hold values from -3 to 3
Outputs:
- decoded: float32 [4, 128, 128, 512], P(None, 'row', 'col', 'section')
Inputs may be any that keep to these rules, and one draw needn't show every extreme that they name: `batch_order`: a permutation of the 4 micro-batches.
All inputs are finite; a program needn't handle non-finite values.
Results may differ from a plain program's by a relative error of at most 0.0025.
Values may be sent and summed in bfloat16 or wider, within the bound.
A program may use at most 128 MiB of HBM per device.

v0:
```python
import jax
import jax.numpy as jnp
from jax import lax
from jax.sharding import PartitionSpec as P

LC = 16
VC = 512
GROUPS = 32
MB = 4
PR = 2
PCOLS = 4
PC = 64


EPSILON = 1e-06


def extended(cells, sides, width):
    for axis, dim in sides:
        count = lax.axis_size(axis)
        ends = count - 1
        head = lax.slice_in_dim(cells, 0, width, axis=dim)
        tail = lax.slice_in_dim(cells, cells.shape[dim] - width, cells.shape[dim], axis=dim)
        cells = jnp.concatenate(
            [
                lax.ppermute(tail, axis, [(i, (i + 1) % count) for i in range(ends)]),
                cells,
                lax.ppermute(head, axis, [((i + 1) % count, i) for i in range(ends)]),
            ],
            axis=dim,
        )
    return cells


def shifted(block, axis, distance):
    devices = range(lax.axis_size(axis))
    route = [(i - distance, i) for i in devices if i - distance in devices]
    return lax.ppermute(block, axis, route)


def tile_conv(padded, kernel, rows_out, cols_out, precision):
    pieces = [
        padded[row_off : row_off + rows_out, col_off : col_off + cols_out, :]
        for row_off in range(3)
        for col_off in range(3)
    ]
    stacked = jnp.concatenate(pieces, axis=-1).reshape(rows_out * cols_out, -1)
    flat_kernel = kernel.reshape(-1, kernel.shape[-1])
    product = jnp.dot(stacked, flat_kernel, preferred_element_type=jnp.float32, precision=precision)
    return product.reshape(rows_out, cols_out, -1)


def double_size(values):
    return jnp.repeat(jnp.repeat(values, 2, axis=0), 2, axis=1)


def shards(
    tokens,
    batch_order,
    modulation,
    expand_weight,
    expand_bias,
    reduce_weight,
    reduce_bias,
    patch_weight,
    patch_bias,
    latent_kernel,
    latent_bias,
    group_gain,
    group_shift,
    decode_kernel,
    decode_bias,
):
    col_count = lax.axis_size("col")
    row_count = lax.axis_size("row")
    col_place = lax.axis_index("col")
    section_place = lax.axis_index("section")
    tower_flag = section_place == 0
    tok_rows = tokens.shape[1]
    part_width = tokens.shape[2]
    full_width = part_width * col_count
    lat_rows = 2 * PR
    lat_cols = 2 * PCOLS
    rim_width = 1
    rim_edge = rim_width - 1
    expand_full, reduce_full = (
        lax.all_gather(expand_weight, "row", axis=0, tiled=True),
        lax.all_gather(reduce_weight, "row", axis=1, tiled=True),
    )

    def run_branch(normed_all):
        hidden = jnp.dot(normed_all, expand_full, preferred_element_type=jnp.float32) + expand_bias
        hidden = jax.nn.gelu(hidden, approximate=True).astype(jnp.bfloat16)
        return jnp.dot(hidden, reduce_full, preferred_element_type=jnp.float32)

    def skip_branch(normed_all):
        return jnp.zeros((tok_rows, full_width), jnp.float32)

    results = []
    carried = jnp.zeros((PR, PCOLS, PC), jnp.float32)
    for section_step in range(MB + 1):
        if section_step >= 1:
            latent = carried / 0.3611 + 0.1159
            latent = (
                latent.reshape(PR, PCOLS, LC, 2, 2)
                .transpose(0, 3, 1, 4, 2)
                .reshape(lat_rows, lat_cols, LC)
            )
            padded_latent = extended(latent, (("row", 0), ("col", 1)), rim_width)
            span_rows = lat_rows + 2 * rim_edge
            span_cols = lat_cols + 2 * rim_edge
            activated = (
                tile_conv(padded_latent, latent_kernel, span_rows, span_cols, lax.Precision.HIGHEST)
                + latent_bias
            )
            grouped = activated.reshape(lat_rows * lat_cols, GROUPS, VC // GROUPS)
            group_sums, group_squares = lax.psum(
                (jnp.sum(grouped, axis=(0, 2)), jnp.sum(grouped * grouped, axis=(0, 2))),
                ("row", "col"),
            )
            cell_count = lat_rows * lat_cols * row_count * col_count * (VC // GROUPS)
            group_mean = group_sums / cell_count
            group_variance = group_squares / cell_count - group_mean * group_mean
            chan_mean = jnp.repeat(group_mean, VC // GROUPS)
            chan_scale = jnp.repeat(lax.rsqrt(group_variance + EPSILON), VC // GROUPS)
            group_normalized = jax.nn.silu(
                (activated - chan_mean) * chan_scale * group_gain + group_shift
            )
            carry_value = extended(
                double_size(group_normalized.astype(jnp.bfloat16)), (("row", 0), ("col", 1)), 1
            )
            passed_over = shifted(carry_value, "section", -1)
            finished_tile = jnp.where(tower_flag, passed_over, carry_value)
            results.append(
                tile_conv(finished_tile, decode_kernel, 2 * lat_rows, 2 * lat_cols, None)
                + decode_bias
            )
        if section_step < MB:
            chosen = batch_order[section_step]
            rows_in = lax.dynamic_index_in_dim(tokens, chosen, 0, keepdims=False)
            factors = lax.dynamic_index_in_dim(modulation, chosen, 0, keepdims=False)
            factors = lax.dynamic_slice_in_dim(factors, col_place * part_width, part_width, 1)
            row_sums, row_squares = lax.psum(
                (jnp.sum(rows_in, axis=1), jnp.sum(rows_in * rows_in, axis=1)), "col"
            )
            row_mean = (row_sums / full_width)[:, None]
            row_var = (row_squares / full_width)[:, None] - row_mean * row_mean
            normed = (
                (rows_in - row_mean) * lax.rsqrt(row_var + EPSILON) * (1.0 + factors[1])
                + factors[0]
            ).astype(jnp.bfloat16)
            tower_normed_all = lax.all_gather(normed, "col", axis=1, tiled=True)
            partial_branch = lax.cond(tower_flag, run_branch, skip_branch, tower_normed_all)
            branch = lax.psum_scatter(partial_branch, "col", scatter_dimension=1, tiled=True)
            residual = rows_in + factors[2] * (branch + reduce_bias)
            final_sums, final_squares = lax.psum(
                (jnp.sum(residual, axis=1), jnp.sum(residual * residual, axis=1)), "col"
            )
            final_mean = (final_sums / full_width)[:, None]
            final_var = (final_squares / full_width)[:, None] - final_mean * final_mean
            final_rows = (residual - final_mean) * lax.rsqrt(final_var + EPSILON) * (
                1.0 + factors[4]
            ) + factors[3]
            local_proj = jnp.dot(
                final_rows,
                patch_weight,
                preferred_element_type=jnp.float32,
                precision=lax.Precision.HIGHEST,
            )
            patches = lax.psum(local_proj, "col")
            patches = patches + patch_bias
            own_block = patches.reshape(PR, col_count, PCOLS, PC)
            carried = shifted(
                lax.dynamic_index_in_dim(own_block, col_place, 1, keepdims=False), "section", 1
            )
    return jnp.stack(results)


def solution(mesh):
    return jax.shard_map(
        shards,
        mesh=mesh,
        in_specs=(
            P(None, "row", "col"),
            P(),
            P(),
            P("row", "col"),
            P("col"),
            P("col", "row"),
            P("col"),
            P("col", None),
            P(),
            P(),
            P(),
            P(),
            P(),
            P(None, None, None, "section"),
            P("section"),
        ),
        out_specs=P(None, "row", "col", "section"),
        check_vma=False,
    )
```

profile of v0, /device:TPU:130, one launch (start us, length us, event | category | flops | bytes accessed | tf_op | source)
XLA Modules:
  0.0 1021.9 jit_solution(18021695075830573317)
XLA Ops:
  16.3 12.3 %all-reduce.3 = (f32[64]{0:T(128)}, f32[64]{0:T(128)}, f32[64]{0:T(128)S(1)}, f32[64]{0:T(128)S(1)}, f32[64]{0:T(128)}, /*index=5*/f32[64]{0:T(128)}, f32[64]{0:T(128)}, f32[64]{0:T(128)}) all-reduce(f32[64]{0:T(128)S(1)} %get-tuple-element.88, f32[64]{0:T(128)S(1)} %get-tuple-element.84, ...), channel_id=1, replica_groups=mesh['section'=2,'row'=16,'col'=8] {'col'}, use_global_device_ids=true, to_apply=%region_57.58 | all-reduce | flops 512 | bytes 4096 | tf_op jit(solution)/shard_map/psum | solution.py:143
  30.6 14.8 %all_gather.22 = bf16[64,3072]{1,0:T(8,128)(2,1)} all-gather(bf16[64,384]{1,0:T(8,128)(2,1)S(1)} %fusion.84), channel_id=1, replica_groups=mesh['section'=2,'row'=16,'col'=8] {'col'}, dimensions={1}, use_global_device_ids=true | all-gather | bytes 442368 | tf_op jit(solution)/shard_map/all_gather | solution.py:152
  45.4 109.7 %all-gather.3.cloned.1.call-done = bf16[3072,1536]{1,0:T(8,128)(2,1)} async-done(((bf16[192,1536]{1,0:T(8,128)(2,1)}), bf16[3072,1536]{1,0:T(8,128)(2,1)}) %all-gather.3.cloned.1.call-update) | async-done | bytes 9437200 | tf_op jit(solution)/shard_map/all_gather | solution.py:87
  155.1 145.7 %all-gather.5.cloned.1.call-done = bf16[1536,3072]{0,1:T(8,128)(2,1)} async-done(((bf16[1536,192]{0,1:T(8,128)(2,1)}), bf16[1536,3072]{0,1:T(8,128)(2,1)}) %all-gather.5.cloned.1.call-update) | async-done | bytes 9437200 | tf_op jit(solution)/shard_map/all_gather | solution.py:88
  300.8 11.1 %conditional.6 = (f32[64,3072]{1,0:T(8,128)S(1)}) conditional(s32[]{:T(128)} %convert_element_type.42, () %tuple.33, (bf16[64,3072]{1,0:T(8,128)(2,1)}, bf16[3072,1536]{1,0:T(8,128)(2,1)}, f32[1536]{0:T(1024)S(1)}, bf16[1536,3072]{0,1:T(8,128)(2,1)}) %tuple.179), branch_computations={%region_40.41_spmd, %region_41.42_spmd} | conditional | flops 1208942592 | bytes 20060168 | solution.py:153
  300.8 11.1 %fusion.44 = f32[64,3072]{1,0:T(8,128)S(1)} fusion(bf16[1536,3072]{0,1:T(8,128)(2,1)} %get-tuple-element.76, bf16[64,3072]{1,0:T(8,128)(2,1)} %get-tuple-element.57, bf16[3072,1536]{1,0:T(8,128)(2,1)} %get-tuple-element.58, f32[1536]{0:T(1024)S(1)} %get-tuple-element.59), kind=kOutput, calls=%fused_computation.50 | convolution fusion | flops 1208942592 | bytes 20060160 | tf_op jit(solution)/shard_map/cond/branch_1_fun/dot_general | solution.py:94
  316.4 14.4 %all_gather.23 = bf16[64,3072]{1,0:T(8,128)(2,1)} all-gather(bf16[64,384]{1,0:T(8,128)(2,1)S(1)} %get-tuple-element.168), channel_id=1, replica_groups=mesh['section'=2,'row'=16,'col'=8] {'col'}, dimensions={1}, use_global_device_ids=true | all-gather | bytes 442368 | tf_op jit(solution)/shard_map/all_gather | solution.py:152
  330.8 11.1 %conditional.7 = (f32[64,3072]{1,0:T(8,128)S(1)}) conditional(s32[]{:T(128)} %convert_element_type.42, () %tuple.35, (bf16[64,3072]{1,0:T(8,128)(2,1)}, bf16[3072,1536]{1,0:T(8,128)(2,1)}, f32[1536]{0:T(1024)S(1)}, bf16[1536,3072]{0,1:T(8,128)(2,1)}) %tuple.180), branch_computations={%region_58.59_spmd, %region_59.60_spmd} | conditional | flops 1208942592 | bytes 20060168 | solution.py:153
  330.8 11.1 %fusion.62 = f32[64,3072]{1,0:T(8,128)S(1)} fusion(bf16[1536,3072]{0,1:T(8,128)(2,1)} %get-tuple-element.80, bf16[64,3072]{1,0:T(8,128)(2,1)} %get-tuple-element.61, bf16[3072,1536]{1,0:T(8,128)(2,1)} %get-tuple-element.62, f32[1536]{0:T(1024)S(1)} %get-tuple-element.63), kind=kOutput, calls=%fused_computation.70 | convolution fusion | flops 1208942592 | bytes 20060160 | tf_op jit(solution)/shard_map/cond/branch_1_fun/dot_general | solution.py:94
  342.9 14.3 %all_gather.21 = bf16[64,3072]{1,0:T(8,128)(2,1)} all-gather(bf16[64,384]{1,0:T(8,128)(2,1)} %get-tuple-element.167), channel_id=1, replica_groups=mesh['section'=2,'row'=16,'col'=8] {'col'}, dimensions={1}, use_global_device_ids=true | all-gather | bytes 442368 | tf_op jit(solution)/shard_map/all_gather | solution.py:152
  357.2 11.2 %conditional.5 = (f32[64,3072]{1,0:T(8,128)S(1)}) conditional(s32[]{:T(128)} %convert_element_type.42, () %tuple.31, (bf16[64,3072]{1,0:T(8,128)(2,1)}, bf16[3072,1536]{1,0:T(8,128)(2,1)}, f32[1536]{0:T(1024)S(1)}, bf16[1536,3072]{0,1:T(8,128)(2,1)}) %tuple.181), branch_computations={%region_22.23_spmd, %region_23.24_spmd} | conditional | flops 1208942592 | bytes 20060168 | solution.py:153
  357.2 11.2 %fusion.26 = f32[64,3072]{1,0:T(8,128)S(1)} fusion(bf16[1536,3072]{0,1:T(8,128)(2,1)} %get-tuple-element.72, bf16[64,3072]{1,0:T(8,128)(2,1)} %get-tuple-element.53, bf16[3072,1536]{1,0:T(8,128)(2,1)} %get-tuple-element.54, f32[1536]{0:T(1024)S(1)} %get-tuple-element.55), kind=kOutput, calls=%fused_computation.30 | convolution fusion | flops 1208942592 | bytes 20060160 | tf_op jit(solution)/shard_map/cond/branch_1_fun/dot_general | solution.py:94
  369.3 14.6 %all_gather.18 = bf16[64,3072]{1,0:T(8,128)(2,1)} all-gather(bf16[64,384]{1,0:T(8,128)(2,1)} %get-tuple-element.166), channel_id=1, replica_groups=mesh['section'=2,'row'=16,'col'=8] {'col'}, dimensions={1}, use_global_device_ids=true | all-gather | bytes 442368 | tf_op jit(solution)/shard_map/all_gather | solution.py:152
  383.9 11.1 %conditional.4 = (f32[64,3072]{1,0:T(8,128)S(1)}) conditional(s32[]{:T(128)} %convert_element_type.42, () %tuple.29, (bf16[64,3072]{1,0:T(8,128)(2,1)}, bf16[3072,1536]{1,0:T(8,128)(2,1)}, f32[1536]{0:T(1024)S(1)}, bf16[1536,3072]{0,1:T(8,128)(2,1)}) %tuple.182), branch_computations={%region_4.5_spmd, %region_5.6_spmd} | conditional | flops 1208942592 | bytes 20060168 | solution.py:153
  383.9 11.1 %fusion.8 = f32[64,3072]{1,0:T(8,128)S(1)} fusion(bf16[1536,3072]{0,1:T(8,128)(2,1)} %get-tuple-element.68, bf16[64,3072]{1,0:T(8,128)(2,1)} %get-tuple-element.42, bf16[3072,1536]{1,0:T(8,128)(2,1)} %get-tuple-element.48, f32[1536]{0:T(1024)S(1)} %get-tuple-element.50), kind=kOutput, calls=%fused_computation.10 | convolution fusion | flops 1208942592 | bytes 20060160 | tf_op jit(solution)/shard_map/cond/branch_1_fun/dot_general | solution.py:94
  396.0 18.3 %reduce-scatter.7.cloned.1.call-done = f32[64,384]{1,0:T(8,128)} async-done(((f32[64,3072]{1,0:T(8,128)}), f32[64,384]{1,0:T(8,128)}) %reduce-scatter.7.cloned.1.call-update) | async-done | bytes 98320 | tf_op jit(solution)/shard_map/reduce_scatter | solution.py:154
  414.3 35.4 %reduce-scatter.5.cloned.1.call-done = f32[64,384]{1,0:T(8,128)} async-done(((f32[64,3072]{1,0:T(8,128)}), f32[64,384]{1,0:T(8,128)}) %reduce-scatter.5.cloned.1.call-update) | async-done | bytes 98320 | tf_op jit(solution)/shard_map/reduce_scatter | solution.py:154
  451.1 13.0 %all-reduce.2 = (f32[64]{0:T(128)S(1)}, f32[64]{0:T(128)S(1)}, f32[64]{0:T(128)S(1)}, f32[64]{0:T(128)S(1)}, f32[64]{0:T(128)S(1)}, /*index=5*/f32[64]{0:T(128)S(1)}, f32[64]{0:T(128)S(1)}, f32[64]{0:T(128)S(1)}) all-reduce(f32[64]{0:T(128)S(1)} %get-tuple-element.163, ...), channel_id=1, replica_groups=mesh['section'=2,'row'=16,'col'=8] {'col'}, use_global_device_ids=true, to_apply=%region_64.65 | all-reduce | flops 512 | bytes 4096 | tf_op jit(solution)/shard_map/psum | solution.py:156
  469.2 64.5 %all-reduce.6.cloned.1.call-done = (f32[64,64]{1,0:T(8,128)}, f32[64,64]{1,0:T(8,128)}, f32[64,64]{1,0:T(8,128)}, f32[64,64]{1,0:T(8,128)}) async-done(((f32[64,64]{1,0:T(8,128)}, f32[64,64]{1,0:T(8,128)}, f32[64,64]{1,0:T(8,128)}, f32[64,64]{1,0:T(8,128)}), (f32[64,64]{1,0:T(8,128)}, f32[64,64]{1,0:T(8,128)}, f32[64,64]{1,0:T(8,128)}, f32[64,64]{1,0:T(8,128)})) %all-reduce.6.cloned.1.call-update) | async-done | bytes 65552 | tf_op jit(solution)/shard_map/psum | solution.py:170
  534.6 3.4 collective-permute-start.10
  542.5 4.6 collective-permute-start.11
  547.1 4.8 collective-permute-start.12
  552.1 2.5 collective-permute-start.21
  554.6 6.9 collective-permute-start.22
  563.8 7.5 collective-permute-start.32
  571.4 1.9 collective-permute-start.1
  573.3 7.5 collective-permute-start.2
  582.9 3.6 collective-permute-start.14
  586.5 1.9 collective-permute-start.23
  588.5 3.6 collective-permute-start.24
  592.2 1.9 collective-permute-start.33
  594.1 3.6 collective-permute-start.34
  600.4 3.6 collective-permute-start.4
  606.9 317.1 %all-reduce = (f32[32]{0:T(128)S(1)}, f32[32]{0:T(128)S(1)}, f32[32]{0:T(128)S(1)}, f32[32]{0:T(128)S(1)}, f32[32]{0:T(128)S(1)}, /*index=5*/f32[32]{0:T(128)S(1)}, f32[32]{0:T(128)S(1)}, f32[32]{0:T(128)S(1)}) all-reduce(f32[32]{0:T(128)S(1)} %reduce_sum.311, ...), channel_id=1, replica_groups=mesh['section'=2,'row'=16,'col'=8] {'row','col'}, use_global_device_ids=true, to_apply=%region_71.72 | all-reduce | flops 256 | bytes 2048 | tf_op jit(solution)/shard_map/psum | solution.py:117
  931.8 7.5 collective-permute-start.6
  939.5 5.4 collective-permute-start.16
  945.2 6.3 collective-permute-start.26
  953.6 7.5 collective-permute-start.36
  961.2 1.9 collective-permute-start.7
  963.2 4.8 collective-permute-start.8
  970.0 6.5 collective-permute-start.18
  978.5 3.6 collective-permute-start.28
  982.2 1.9 collective-permute-start.37
  984.3 3.6 collective-permute-start.38
  993.7 5.0 collective-permute-done.9
  998.7 5.3 collective-permute-done.19
  1006.3 3.0 collective-permute-done.29
  1009.2 3.0 collective-permute-done.39
  (302 shorter events, 57.6 us)
Async XLA Ops:
  6.5 998.4 %copy-start = (bf16[3,3,512,256]{3,2,1,0:T(8,128)(2,1)S(1)}, bf16[3,3,512,256]{3,2,1,0:T(8,128)(2,1)}, u32[]{:S(2)}) copy-start(bf16[3,3,512,256]{3,2,1,0:T(8,128)(2,1)} %param.36) | copy-start | bytes 7077892
  6.5 148.6 %all-gather.3.cloned.1.call-start = ((), (), s32[]{:S(2)}) async-start(), calls=%async_computation.4 | async-start | bytes 10027008 | tf_op jit(solution)/shard_map/all_gather | solution.py:87
  7.3 293.6 %all-gather.5.cloned.1.call-start = ((), (), s32[]{:S(2)}) async-start(), calls=%async_computation.5 | async-start | bytes 10027008 | tf_op jit(solution)/shard_map/all_gather | solution.py:88
  8.0 387.9 %reduce-scatter.9.cloned.1.call-start = ((), (), s32[]{:S(2)}) async-start(), calls=%async_computation.8 | async-start | bytes 884736 | tf_op jit(solution)/shard_map/reduce_scatter | solution.py:154
  312.8 83.1 %reduce-scatter.11.cloned.1.call-start = ((), (), s32[]{:S(2)}) async-start(), calls=%async_computation.9 | async-start | bytes 884736 | tf_op jit(solution)/shard_map/reduce_scatter | solution.py:154
  342.8 71.4 %reduce-scatter.7.cloned.1.call-start = ((), (), s32[]{:S(2)}) async-start(), calls=%async_computation.7 | async-start | bytes 884736 | tf_op jit(solution)/shard_map/reduce_scatter | solution.py:154
  369.3 80.4 %reduce-scatter.5.cloned.1.call-start = ((), (), s32[]{:S(2)}) async-start(), calls=%async_computation.6 | async-start | bytes 884736 | tf_op jit(solution)/shard_map/reduce_scatter | solution.py:154
  395.9 137.8 %all-reduce.6.cloned.1.call-start = ((), (), s32[]{:S(2)}) async-start(), calls=%async_computation.10 | async-start | bytes 262144 | tf_op jit(solution)/shard_map/psum | solution.py:170
  534.6 7.7 collective-permute-start.10
  538.2 13.8 %collective-permute-start.20 = (f32[2,4,64]{1,2,0:T(8,128)S(1)}, f32[2,4,64]{1,2,0:T(8,128)S(1)}, u32[]{:S(2)}, u32[]{:S(2)}) collective-permute-start(f32[2,4,64]{1,2,0:T(8,128)S(1)} %bitcast.196), channel_id=1, source_target_pairs={{0,128},{1,129},{2,130},{3,131},{4,132},{5,133},{6,134},{7,135},{8... | collective-permute-start | bytes 6152 | tf_op jit(solution)/shard_map/ppermute | solution.py:38
  539.6 15.0 %collective-permute-start.30 = (f32[2,4,64]{1,2,0:T(8,128)S(1)}, f32[2,4,64]{1,2,0:T(8,128)S(1)}, u32[]{:S(2)}, u32[]{:S(2)}) collective-permute-start(f32[2,4,64]{1,2,0:T(8,128)S(1)} %bitcast.195), channel_id=1, source_target_pairs={{0,128},{1,129},{2,130},{3,131},{4,132},{5,133},{6,134},{7,135},{8... | collective-permute-start | bytes 6152 | tf_op jit(solution)/shard_map/ppermute | solution.py:38
  541.0 20.7 %collective-permute-start = (f32[2,4,64]{1,2,0:T(8,128)S(1)}, f32[2,4,64]{1,2,0:T(8,128)S(1)}, u32[]{:S(2)}, u32[]{:S(2)}) collective-permute-start(f32[2,4,64]{1,2,0:T(8,128)S(1)} %bitcast.194), channel_id=1, source_target_pairs={{0,128},{1,129},{2,130},{3,131},{4,132},{5,133},{6,134},{7,135},{8... | collective-permute-start | bytes 6152 | tf_op jit(solution)/shard_map/ppermute | solution.py:38
  542.5 21.3 %collective-permute-start.11 = (f32[1,8,16]{2,1,0:T(8,128)S(1)}, f32[1,8,16]{2,1,0:T(8,128)S(1)}, u32[]{:S(2)}, u32[]{:S(2)}) collective-permute-start(f32[1,8,16]{2,1,0:T(8,128)S(1)} %get-tuple-element.231), channel_id=1, source_target_pairs={{0,8},{8,16},{16,24},{24,32},{32,40},{40,48},{48,56},{56,64},{64,7... | collective-permute-start | bytes 1544 | tf_op jit(solution)/shard_map/ppermute | solution.py:26
  547.1 24.2 %collective-permute-start.12 = (f32[1,8,16]{2,1,0:T(8,128)S(1)}, f32[1,8,16]{2,1,0:T(8,128)S(1)}, u32[]{:S(2)}, u32[]{:S(2)}) collective-permute-start(f32[1,8,16]{2,1,0:T(8,128)S(1)} %get-tuple-element.232), channel_id=1, source_target_pairs={{8,0},{16,8},{24,16},{32,24},{40,32},{48,40},{56,48},{64,56},{72,6... | collective-permute-start | bytes 1544 | tf_op jit(solution)/shard_map/ppermute | solution.py:28
  552.1 21.2 %collective-permute-start.21 = (f32[1,8,16]{2,1,0:T(8,128)S(1)}, f32[1,8,16]{2,1,0:T(8,128)S(1)}, u32[]{:S(2)}, u32[]{:S(2)}) collective-permute-start(f32[1,8,16]{2,1,0:T(8,128)S(1)} %get-tuple-element.235), channel_id=1, source_target_pairs={{0,8},{8,16},{16,24},{24,32},{32,40},{40,48},{48,56},{56,64},{64,7... | collective-permute-start | bytes 1544 | tf_op jit(solution)/shard_map/ppermute | solution.py:26
  554.6 26.2 %collective-permute-start.22 = (f32[1,8,16]{2,1,0:T(8,128)S(1)}, f32[1,8,16]{2,1,0:T(8,128)S(1)}, u32[]{:S(2)}, u32[]{:S(2)}) collective-permute-start(f32[1,8,16]{2,1,0:T(8,128)S(1)} %get-tuple-element.236), channel_id=1, source_target_pairs={{8,0},{16,8},{24,16},{32,24},{40,32},{48,40},{56,48},{64,56},{72,6... | collective-permute-start | bytes 1544 | tf_op jit(solution)/shard_map/ppermute | solution.py:28
  561.7 21.1 %collective-permute-start.31 = (f32[1,8,16]{2,1,0:T(8,128)S(1)}, f32[1,8,16]{2,1,0:T(8,128)S(1)}, u32[]{:S(2)}, u32[]{:S(2)}) collective-permute-start(f32[1,8,16]{2,1,0:T(8,128)S(1)} %get-tuple-element.239), channel_id=1, source_target_pairs={{0,8},{8,16},{16,24},{24,32},{32,40},{40,48},{48,56},{56,64},{64,7... | collective-permute-start | bytes 1544 | tf_op jit(solution)/shard_map/ppermute | solution.py:26
  563.8 22.7 %collective-permute-start.32 = (f32[1,8,16]{2,1,0:T(8,128)S(1)}, f32[1,8,16]{2,1,0:T(8,128)S(1)}, u32[]{:S(2)}, u32[]{:S(2)}) collective-permute-start(f32[1,8,16]{2,1,0:T(8,128)S(1)} %get-tuple-element.240), channel_id=1, source_target_pairs={{8,0},{16,8},{24,16},{32,24},{40,32},{48,40},{56,48},{64,56},{72,6... | collective-permute-start | bytes 1544 | tf_op jit(solution)/shard_map/ppermute | solution.py:28
  571.4 17.1 %collective-permute-start.1 = (f32[1,8,16]{2,1,0:T(8,128)S(1)}, f32[1,8,16]{2,1,0:T(8,128)S(1)}, u32[]{:S(2)}, u32[]{:S(2)}) collective-permute-start(f32[1,8,16]{2,1,0:T(8,128)S(1)} %get-tuple-element.227), channel_id=1, source_target_pairs={{0,8},{8,16},{16,24},{24,32},{32,40},{40,48},{48,56},{56,64},{64,7... | collective-permute-start | bytes 1544 | tf_op jit(solution)/shard_map/ppermute | solution.py:26
  573.3 18.8 %collective-permute-start.2 = (f32[1,8,16]{2,1,0:T(8,128)S(1)}, f32[1,8,16]{2,1,0:T(8,128)S(1)}, u32[]{:S(2)}, u32[]{:S(2)}) collective-permute-start(f32[1,8,16]{2,1,0:T(8,128)S(1)} %get-tuple-element.228), channel_id=1, source_target_pairs={{8,0},{16,8},{24,16},{32,24},{40,32},{48,40},{56,48},{64,56},{72,6... | collective-permute-start | bytes 1544 | tf_op jit(solution)/shard_map/ppermute | solution.py:28
  580.9 13.2 %collective-permute-start.13 = (f32[6,1,16]{2,1,0:T(1,128)S(1)}, f32[6,1,16]{2,1,0:T(1,128)S(1)}, u32[]{:S(2)}, u32[]{:S(2)}) collective-permute-start(f32[6,1,16]{2,1,0:T(1,128)S(1)} %get-tuple-element.216), channel_id=1, source_target_pairs={{0,1},{1,2},{2,3},{3,4},{4,5},{5,6},{6,7},{8,9},{9,10},{10,11},{11... | collective-permute-start | bytes 1160 | tf_op jit(solution)/shard_map/ppermute | solution.py:26
  582.9 14.9 %collective-permute-start.14 = (f32[6,1,16]{2,1,0:T(1,128)S(1)}, f32[6,1,16]{2,1,0:T(1,128)S(1)}, u32[]{:S(2)}, u32[]{:S(2)}) collective-permute-start(f32[6,1,16]{2,1,0:T(1,128)S(1)} %get-tuple-element.215), channel_id=1, source_target_pairs={{1,0},{2,1},{3,2},{4,3},{5,4},{6,5},{7,6},{9,8},{10,9},{11,10},{12... | collective-permute-start | bytes 1160 | tf_op jit(solution)/shard_map/ppermute | solution.py:28
  586.5 13.8 %collective-permute-start.23 = (f32[6,1,16]{2,1,0:T(1,128)S(1)}, f32[6,1,16]{2,1,0:T(1,128)S(1)}, u32[]{:S(2)}, u32[]{:S(2)}) collective-permute-start(f32[6,1,16]{2,1,0:T(1,128)S(1)} %get-tuple-element.220), channel_id=1, source_target_pairs={{0,1},{1,2},{2,3},{3,4},{4,5},{5,6},{6,7},{8,9},{9,10},{10,11},{11... | collective-permute-start | bytes 1160 | tf_op jit(solution)/shard_map/ppermute | solution.py:26
  588.5 15.5 %collective-permute-start.24 = (f32[6,1,16]{2,1,0:T(1,128)S(1)}, f32[6,1,16]{2,1,0:T(1,128)S(1)}, u32[]{:S(2)}, u32[]{:S(2)}) collective-permute-start(f32[6,1,16]{2,1,0:T(1,128)S(1)} %get-tuple-element.219), channel_id=1, source_target_pairs={{1,0},{2,1},{3,2},{4,3},{5,4},{6,5},{7,6},{9,8},{10,9},{11,10},{12... | collective-permute-start | bytes 1160 | tf_op jit(solution)/shard_map/ppermute | solution.py:28
  592.2 12.8 %collective-permute-start.33 = (f32[6,1,16]{2,1,0:T(1,128)S(1)}, f32[6,1,16]{2,1,0:T(1,128)S(1)}, u32[]{:S(2)}, u32[]{:S(2)}) collective-permute-start(f32[6,1,16]{2,1,0:T(1,128)S(1)} %get-tuple-element.224), channel_id=1, source_target_pairs={{0,1},{1,2},{2,3},{3,4},{4,5},{5,6},{6,7},{8,9},{9,10},{10,11},{11... | collective-permute-start | bytes 1160 | tf_op jit(solution)/shard_map/ppermute | solution.py:26
  594.1 10.9 %collective-permute-start.34 = (f32[6,1,16]{2,1,0:T(1,128)S(1)}, f32[6,1,16]{2,1,0:T(1,128)S(1)}, u32[]{:S(2)}, u32[]{:S(2)}) collective-permute-start(f32[6,1,16]{2,1,0:T(1,128)S(1)} %get-tuple-element.223), channel_id=1, source_target_pairs={{1,0},{2,1},{3,2},{4,3},{5,4},{6,5},{7,6},{9,8},{10,9},{11,10},{12... | collective-permute-start | bytes 1160 | tf_op jit(solution)/shard_map/ppermute | solution.py:28
  597.8 8.2 collective-permute-start.3
  600.4 5.6 collective-permute-start.4
  925.5 19.7 %collective-permute-start.5 = (bf16[1,16,512]{2,1,0:T(8,128)(2,1)S(1)}, bf16[1,16,512]{2,1,0:T(8,128)(2,1)S(1)}, u32[]{:S(2)}, u32[]{:S(2)}) collective-permute-start(bf16[1,16,512]{2,1,0:T(8,128)(2,1)S(1)} %broadcast_in_dim.136), channel_id=1, source_target_pairs={{0,8},{8,16},{16,24},{24,32},{32,40},{40,48},{48,56},{56,64},{64,7... | collective-permute-start | bytes 49160 | tf_op jit(solution)/shard_map/ppermute | solution.py:26
  927.5 26.1 %collective-permute-start.15 = (bf16[1,16,512]{2,1,0:T(8,128)(2,1)S(1)}, bf16[1,16,512]{2,1,0:T(8,128)(2,1)S(1)}, u32[]{:S(2)}, u32[]{:S(2)}) collective-permute-start(bf16[1,16,512]{2,1,0:T(8,128)(2,1)S(1)} %broadcast_in_dim.144), channel_id=1, source_target_pairs={{0,8},{8,16},{16,24},{24,32},{32,40},{40,48},{48,56},{56,64},{64,7... | collective-permute-start | bytes 49160 | tf_op jit(solution)/shard_map/ppermute | solution.py:26
  929.6 33.5 %collective-permute-start.25 = (bf16[1,16,512]{2,1,0:T(8,128)(2,1)S(1)}, bf16[1,16,512]{2,1,0:T(8,128)(2,1)S(1)}, u32[]{:S(2)}, u32[]{:S(2)}) collective-permute-start(bf16[1,16,512]{2,1,0:T(8,128)(2,1)S(1)} %broadcast_in_dim.152), channel_id=1, source_target_pairs={{0,8},{8,16},{16,24},{24,32},{32,40},{40,48},{48,56},{56,64},{64,7... | collective-permute-start | bytes 49160 | tf_op jit(solution)/shard_map/ppermute | solution.py:26
  931.8 19.8 %collective-permute-start.6 = (bf16[1,16,512]{2,1,0:T(8,128)(2,1)S(1)}, bf16[1,16,512]{2,1,0:T(8,128)(2,1)S(1)}, u32[]{:S(2)}, u32[]{:S(2)}) collective-permute-start(bf16[1,16,512]{2,1,0:T(8,128)(2,1)S(1)} %broadcast_in_dim.139), channel_id=1, source_target_pairs={{8,0},{16,8},{24,16},{32,24},{40,32},{48,40},{56,48},{64,56},{72,6... | collective-permute-start | bytes 49160 | tf_op jit(solution)/shard_map/ppermute | solution.py:28
  939.5 21.7 %collective-permute-start.16 = (bf16[1,16,512]{2,1,0:T(8,128)(2,1)S(1)}, bf16[1,16,512]{2,1,0:T(8,128)(2,1)S(1)}, u32[]{:S(2)}, u32[]{:S(2)}) collective-permute-start(bf16[1,16,512]{2,1,0:T(8,128)(2,1)S(1)} %broadcast_in_dim.147), channel_id=1, source_target_pairs={{8,0},{16,8},{24,16},{32,24},{40,32},{48,40},{56,48},{64,56},{72,6... | collective-permute-start | bytes 49160 | tf_op jit(solution)/shard_map/ppermute | solution.py:28
  945.2 22.8 %collective-permute-start.26 = (bf16[1,16,512]{2,1,0:T(8,128)(2,1)S(1)}, bf16[1,16,512]{2,1,0:T(8,128)(2,1)S(1)}, u32[]{:S(2)}, u32[]{:S(2)}) collective-permute-start(bf16[1,16,512]{2,1,0:T(8,128)(2,1)S(1)} %broadcast_in_dim.155), channel_id=1, source_target_pairs={{8,0},{16,8},{24,16},{32,24},{40,32},{48,40},{56,48},{64,56},{72,6... | collective-permute-start | bytes 49160 | tf_op jit(solution)/shard_map/ppermute | solution.py:28
  951.6 18.4 %collective-permute-start.35 = (bf16[1,16,512]{2,1,0:T(8,128)(2,1)S(1)}, bf16[1,16,512]{2,1,0:T(8,128)(2,1)S(1)}, u32[]{:S(2)}, u32[]{:S(2)}) collective-permute-start(bf16[1,16,512]{2,1,0:T(8,128)(2,1)S(1)} %broadcast_in_dim.160), channel_id=1, source_target_pairs={{0,8},{8,16},{16,24},{24,32},{32,40},{40,48},{48,56},{56,64},{64,7... | collective-permute-start | bytes 49160 | tf_op jit(solution)/shard_map/ppermute | solution.py:26
  953.6 23.0 %collective-permute-start.36 = (bf16[1,16,512]{2,1,0:T(8,128)(2,1)S(1)}, bf16[1,16,512]{2,1,0:T(8,128)(2,1)S(1)}, u32[]{:S(2)}, u32[]{:S(2)}) collective-permute-start(bf16[1,16,512]{2,1,0:T(8,128)(2,1)S(1)} %broadcast_in_dim.163), channel_id=1, source_target_pairs={{8,0},{16,8},{24,16},{32,24},{40,32},{48,40},{56,48},{64,56},{72,6... | collective-permute-start | bytes 49160 | tf_op jit(solution)/shard_map/ppermute | solution.py:28
  961.2 17.4 %collective-permute-start.7 = (bf16[10,1,512]{2,1,0:T(2,128)(2,1)S(1)}, bf16[10,1,512]{2,1,0:T(2,128)(2,1)S(1)}, u32[]{:S(2)}, u32[]{:S(2)}) collective-permute-start(bf16[10,1,512]{2,1,0:T(2,128)(2,1)S(1)} %get-tuple-element.169), channel_id=1, source_target_pairs={{0,1},{1,2},{2,3},{3,4},{4,5},{5,6},{6,7},{8,9},{9,10},{10,11},{11... | collective-permute-start | bytes 30728 | tf_op jit(solution)/shard_map/ppermute | solution.py:26
  963.2 19.0 %collective-permute-start.8 = (bf16[10,1,512]{2,1,0:T(2,128)(2,1)S(1)}, bf16[10,1,512]{2,1,0:T(2,128)(2,1)S(1)}, u32[]{:S(2)}, u32[]{:S(2)}) collective-permute-start(bf16[10,1,512]{2,1,0:T(2,128)(2,1)S(1)} %get-tuple-element.170), channel_id=1, source_target_pairs={{1,0},{2,1},{3,2},{4,3},{5,4},{6,5},{7,6},{9,8},{10,9},{11,10},{12... | collective-permute-start | bytes 30728 | tf_op jit(solution)/shard_map/ppermute | solution.py:28
  968.0 16.2 %collective-permute-start.17 = (bf16[10,1,512]{2,1,0:T(2,128)(2,1)S(1)}, bf16[10,1,512]{2,1,0:T(2,128)(2,1)S(1)}, u32[]{:S(2)}, u32[]{:S(2)}) collective-permute-start(bf16[10,1,512]{2,1,0:T(2,128)(2,1)S(1)} %get-tuple-element.171), channel_id=1, source_target_pairs={{0,1},{1,2},{2,3},{3,4},{4,5},{5,6},{6,7},{8,9},{9,10},{10,11},{11... | collective-permute-start | bytes 30728 | tf_op jit(solution)/shard_map/ppermute | solution.py:26
  970.0 17.9 %collective-permute-start.18 = (bf16[10,1,512]{2,1,0:T(2,128)(2,1)S(1)}, bf16[10,1,512]{2,1,0:T(2,128)(2,1)S(1)}, u32[]{:S(2)}, u32[]{:S(2)}) collective-permute-start(bf16[10,1,512]{2,1,0:T(2,128)(2,1)S(1)} %get-tuple-element.172), channel_id=1, source_target_pairs={{1,0},{2,1},{3,2},{4,3},{5,4},{6,5},{7,6},{9,8},{10,9},{11,10},{12... | collective-permute-start | bytes 30728 | tf_op jit(solution)/shard_map/ppermute | solution.py:28
  976.5 12.8 %collective-permute-start.27 = (bf16[10,1,512]{2,1,0:T(2,128)(2,1)S(1)}, bf16[10,1,512]{2,1,0:T(2,128)(2,1)S(1)}, u32[]{:S(2)}, u32[]{:S(2)}) collective-permute-start(bf16[10,1,512]{2,1,0:T(2,128)(2,1)S(1)} %get-tuple-element.173), channel_id=1, source_target_pairs={{0,1},{1,2},{2,3},{3,4},{4,5},{5,6},{6,7},{8,9},{9,10},{10,11},{11... | collective-permute-start | bytes 30728 | tf_op jit(solution)/shard_map/ppermute | solution.py:26
  978.5 12.1 %collective-permute-start.28 = (bf16[10,1,512]{2,1,0:T(2,128)(2,1)S(1)}, bf16[10,1,512]{2,1,0:T(2,128)(2,1)S(1)}, u32[]{:S(2)}, u32[]{:S(2)}) collective-permute-start(bf16[10,1,512]{2,1,0:T(2,128)(2,1)S(1)} %get-tuple-element.174), channel_id=1, source_target_pairs={{1,0},{2,1},{3,2},{4,3},{5,4},{6,5},{7,6},{9,8},{10,9},{11,10},{12... | collective-permute-start | bytes 30728 | tf_op jit(solution)/shard_map/ppermute | solution.py:28
  982.2 9.9 collective-permute-start.37
  984.3 7.8 collective-permute-start.38
  987.9 10.8 %collective-permute-start.9 = (bf16[10,18,512]{2,1,0:T(8,128)(2,1)S(1)}, bf16[10,18,512]{2,1,0:T(8,128)(2,1)S(1)}, u32[]{:S(2)}, u32[]{:S(2)}) collective-permute-start(bf16[10,18,512]{2,1,0:T(8,128)(2,1)S(1)} %pad_maximum_fusion.1), channel_id=1, source_target_pairs={{128,0},{129,1},{130,2},{131,3},{132,4},{133,5},{134,6},{135,7},{1... | collective-permute-start | bytes 552968 | tf_op jit(solution)/shard_map/ppermute | solution.py:38
  989.3 14.6 %collective-permute-start.19 = (bf16[10,18,512]{2,1,0:T(8,128)(2,1)S(1)}, bf16[10,18,512]{2,1,0:T(8,128)(2,1)S(1)}, u32[]{:S(2)}, u32[]{:S(2)}) collective-permute-start(bf16[10,18,512]{2,1,0:T(8,128)(2,1)S(1)} %pad_maximum_fusion.2), channel_id=1, source_target_pairs={{128,0},{129,1},{130,2},{131,3},{132,4},{133,5},{134,6},{135,7},{1... | collective-permute-start | bytes 552968 | tf_op jit(solution)/shard_map/ppermute | solution.py:38
  990.8 18.5 %collective-permute-start.29 = (bf16[10,18,512]{2,1,0:T(8,128)(2,1)S(1)}, bf16[10,18,512]{2,1,0:T(8,128)(2,1)S(1)}, u32[]{:S(2)}, u32[]{:S(2)}) collective-permute-start(bf16[10,18,512]{2,1,0:T(8,128)(2,1)S(1)} %pad_maximum_fusion.3), channel_id=1, source_target_pairs={{128,0},{129,1},{130,2},{131,3},{132,4},{133,5},{134,6},{135,7},{1... | collective-permute-start | bytes 552968 | tf_op jit(solution)/shard_map/ppermute | solution.py:38
  992.2 20.1 %collective-permute-start.39 = (bf16[10,18,512]{2,1,0:T(8,128)(2,1)S(1)}, bf16[10,18,512]{2,1,0:T(8,128)(2,1)S(1)}, u32[]{:S(2)}, u32[]{:S(2)}) collective-permute-start(bf16[10,18,512]{2,1,0:T(8,128)(2,1)S(1)} %pad_maximum_fusion.4), channel_id=1, source_target_pairs={{128,0},{129,1},{130,2},{131,3},{132,4},{133,5},{134,6},{135,7},{1... | collective-permute-start | bytes 552968 | tf_op jit(solution)/shard_map/ppermute | solution.py:38
  (16 other events, 1378.7 us)
Sparse Core Ops, SparseCore 0:
  10.0 145.1 all-gather.2
  157.7 143.0 all-gather.4
  313.0 30.0 reduce-scatter.8
  345.7 32.7 reduce-scatter.10
  380.8 33.4 reduce-scatter.6
  416.8 32.8 reduce-scatter.4
  469.3 64.3 all-reduce.5
where the time goes:
time: 1020 us
  blocking collectives  400 us (39%)
  waiting for transfers between devices  391 us (38%)
  starting transfers between devices  134 us (13%)
  matrix products  52.6 us (5%)
  between operations  22.6 us (2%)
  other arithmetic  11.2 us (1%)
    psum x1, blocking collectives, shards(): lax.psum((jnp.sum(grouped, axis=(0, 2)), jnp.sum(grouped * grouped, axis=...  317 us
    all_gather x1, waiting for transfers between devices, shards(): lax.all_gather(reduce_weight, 'row', axis=1, tiled=True)  146 us
    all_gather x1, waiting for transfers between devices, shards(): lax.all_gather(expand_weight, 'row', axis=0, tiled=True)  110 us
    ppermute x16, starting transfers between devices, extended(): lax.ppermute(head, axis, [((i + 1) % count, i) for i in range(ends)])  86.8 us
    psum x1, waiting for transfers between devices, shards(): patches = lax.psum(local_proj, 'col')  64.5 us
    all_gather x4, blocking collectives, shards(): tower_normed_all = lax.all_gather(normed, 'col', axis=1, tiled=True)  58.1 us
    reduce_scatter x4, waiting for transfers between devices, shards(): lax.psum_scatter(partial_branch, 'col', scatter_dimension=1, tiled=True)  53.8 us
    dot_general x4, matrix products, run_branch(): return jnp.dot(hidden, reduce_full, preferred_element_type=jnp.float32)  44.5 us
  transfers between devices with their start and end apart: 47, of which 9 were waited for; matrix products, arithmetic and copies ran while one was open for 5% of the time, Pallas kernels for 0%

commit v1 on v0

v1 whole, which is shorter than its diff:
```python
import functools

import jax
import jax.numpy as jnp
from jax import lax
from jax.experimental import pallas as pl
from jax.experimental.pallas import tpu as pltpu
from jax.sharding import PartitionSpec as P

MESH = pl.DeviceIdType.MESH
EPSILON = 1e-06
N_ROW = 16
N_COL = 8
CELLS = 64 * 64 * 16
LC = 16
MB = 4
PR = 2
PCOLS = 4
PC = 64


def phase_of(base, step):
    if base == 0:
        return [(1, 0), (0, 0), (1, 1)][step + 1]
    return [(0, 0), (1, 1), (0, 1)][step + 1]


def decoder_kernel(
    lat_ref,
    lk_ref,
    lb_ref,
    gain_ref,
    shift_ref,
    dk_ref,
    db_ref,
    out_ref,
    blocks,
    patches,
    weights,
    act,
    cells,
    products,
    col_stats,
    row_stats,
    halo_send,
    halo_recv,
    col_send,
    col_recv,
    row_send,
    row_recv,
):
    s = lax.axis_index("section")
    r = lax.axis_index("row")
    c = lax.axis_index("col")

    halo = []
    for ds in range(2):
        for dr in (-1, 0, 1):
            for dc in (-1, 0, 1):
                if (ds, dr, dc) != (0, 0, 0):
                    halo.append((ds, dr, dc))

    def place(ds, dr, dc):
        return (
            lax.rem(s + ds, 2),
            lax.rem(r + dr + N_ROW, N_ROW),
            lax.rem(c + dc + N_COL, N_COL),
        )

    barrier = pltpu.get_barrier_semaphore()
    greeted = 0
    for ds, dr, dc in halo:
        pl.semaphore_signal(barrier, inc=1, device_id=place(ds, dr, dc), device_id_type=MESH)
        greeted += 1
    for dc in range(2, N_COL - 1):
        pl.semaphore_signal(barrier, inc=1, device_id=place(0, 0, dc), device_id_type=MESH)
        greeted += 1
    for dr in range(2, N_ROW - 1):
        pl.semaphore_signal(barrier, inc=1, device_id=place(0, dr, 0), device_id_type=MESH)
        greeted += 1
    blocks[1, 1, s] = lat_ref[...]
    pl.semaphore_wait(barrier, greeted)

    copies = []
    for i, (ds, dr, dc) in enumerate(halo):
        copy = pltpu.make_async_remote_copy(
            src_ref=lat_ref,
            dst_ref=blocks.at[1 - dr, 1 - dc, s],
            send_sem=halo_send.at[ds, 1 - dr, 1 - dc],
            recv_sem=halo_recv.at[ds, 1 - dr, 1 - dc],
            device_id=place(ds, dr, dc),
            device_id_type=MESH,
        )
        copy.start()
        copies.append(copy)

    weights[...] = jnp.zeros_like(weights)
    for u in range(2):
        for v in range(2):
            for sa in range(2):
                for sb in range(2):
                    for a in range(2):
                        for b in range(2):
                            di = 2 * u + sa - 2 + a
                            dj = 2 * v + sb - 2 + b
                            if abs(di) <= 1 and abs(dj) <= 1:
                                row = ((u * 2 + v) * 2 + sa) * 2 + sb
                                tap = lk_ref[di + 1, dj + 1]
                                high = tap.astype(jnp.bfloat16)
                                low = (tap - high.astype(jnp.float32)).astype(jnp.bfloat16)
                                phase = 2 * a + b
                                rows = pl.ds(row * 16, 16)
                                lanes = pl.ds(phase * 512, 512)
                                weights[0, rows, lanes] = high
                                weights[1, rows, lanes] = low
    patches[...] = jnp.zeros_like(patches)

    for copy in copies:
        copy.wait()

    for ds in range(2):
        for dr in (-1, 0, 1):
            for dc in (-1, 0, 1):
                inside = (r + dr >= 0) & (r + dr < N_ROW) & (c + dc >= 0) & (c + dc < N_COL)
                keep = jnp.where(inside, 1.0, 0.0).astype(jnp.float32)
                block = blocks[dr + 1, dc + 1, ds][:, :64] * keep
                rows = {-1: ((1, 0),), 0: ((0, 1), (1, 2)), 1: ((0, 3),)}[dr]
                first, count, at = {-1: (3, 1, 0), 0: (0, 4, 1), 1: (0, 1, 5)}[dc]
                for mb in range(2):
                    for source, target in rows:
                        start = mb * 8 + source * 4 + first
                        patches[2 * ds + mb, target, at : at + count, :] = block[
                            start : start + count
                        ]

    slabs = [
        patches[:, u : u + 3, v : v + 8, :].reshape(96, 64) for u in range(2) for v in range(2)
    ]
    window = jnp.concatenate(slabs, axis=-1)
    high = window.astype(jnp.bfloat16)
    low = (window - high.astype(jnp.float32)).astype(jnp.bfloat16)
    both = jnp.concatenate([high, low], axis=0)

    jj = lax.broadcasted_iota(jnp.int32, (96, 1), 0) % 8
    ii = (lax.broadcasted_iota(jnp.int32, (96, 1), 0) // 8) % 3
    sums = jnp.zeros((4, 512), jnp.float32)
    squares = jnp.zeros((4, 512), jnp.float32)
    for a in range(2):
        for b in range(2):
            phase = 2 * a + b
            lanes = pl.ds(phase * 512, 512)
            first = jnp.dot(both, weights[0, :, lanes], preferred_element_type=jnp.float32)
            second = jnp.dot(high, weights[1, :, lanes], preferred_element_type=jnp.float32)
            value = first[:96] + (first[96:] + second) + lb_ref[...]
            act[phase] = value
            own = (ii >= a) & (ii < a + 2) & (jj >= b) & (jj < b + 4)
            masked = jnp.where(own, value, 0.0).reshape(4, 24, 512)
            sums += jnp.sum(masked, axis=1)
            squares += jnp.sum(masked * masked, axis=1)

    chan = lax.broadcasted_iota(jnp.int32, (512, 128), 0) // 16
    member = (chan == lax.broadcasted_iota(jnp.int32, (512, 128), 1)).astype(jnp.float32)
    chan_t = lax.broadcasted_iota(jnp.int32, (128, 512), 1) // 16
    member_t = (chan_t == lax.broadcasted_iota(jnp.int32, (128, 512), 0)).astype(jnp.float32)
    stats = jnp.dot(
        jnp.concatenate([sums, squares], axis=0),
        member,
        preferred_element_type=jnp.float32,
        precision=lax.Precision.HIGHEST,
    )

    col_stats[c] = stats
    copies = []
    for dc in range(1, N_COL):
        copy = pltpu.make_async_remote_copy(
            src_ref=col_stats.at[c],
            dst_ref=col_stats.at[c],
            send_sem=col_send.at[dc],
            recv_sem=col_recv.at[dc],
            device_id=place(0, 0, dc),
            device_id_type=MESH,
        )
        copy.start()
        copies.append(copy)
    for copy in copies:
        copy.wait()
    row_stats[r] = jnp.sum(col_stats[...], axis=0)
    copies = []
    for dr in range(1, N_ROW):
        copy = pltpu.make_async_remote_copy(
            src_ref=row_stats.at[r],
            dst_ref=row_stats.at[r],
            send_sem=row_send.at[dr],
            recv_sem=row_recv.at[dr],
            device_id=place(0, dr, 0),
            device_id_type=MESH,
        )
        copy.start()
        copies.append(copy)
    for copy in copies:
        copy.wait()
    total = jnp.sum(row_stats[...], axis=0) * (1.0 / CELLS)
    mean = total[:4]
    scale = lax.rsqrt(total[4:] - mean * mean + EPSILON)
    spread = jnp.dot(
        jnp.concatenate([mean, scale], axis=0),
        member_t,
        preferred_element_type=jnp.float32,
        precision=lax.Precision.HIGHEST,
    )

    for a in range(2):
        for b in range(2):
            phase = 2 * a + b
            line = 4 * r + 2 * ii - a
            across = 8 * c + 2 * jj - b
            inside = (line >= 0) & (line < 64) & (across >= 0) & (across < 64)
            parts = []
            for mb in range(4):
                value = act[phase, mb * 24 : mb * 24 + 24]
                value = (value - spread[mb : mb + 1]) * (
                    spread[4 + mb : 5 + mb] * gain_ref[...]
                ) + shift_ref[...]
                parts.append(value / (1.0 + jnp.exp(-value)))
            value = jnp.where(inside, jnp.concatenate(parts, axis=0), 0.0)
            cells[phase * 96 : phase * 96 + 96, :] = value.astype(jnp.bfloat16)

    for tap in range(9):
        value = jnp.dot(cells[...], dk_ref[tap], preferred_element_type=jnp.float32)
        products[tap] = value.reshape(4, 4, 3, 8, 256)

    for a in range(2):
        for b in range(2):
            for up in range(2):
                for left in range(2):
                    total = jnp.zeros((4, 2, 4, 256), jnp.float32) + db_ref[...]
                    for di in range(3):
                        row_phase, row_at = phase_of(a, (up + di - 1) // 2)
                        for dj in range(3):
                            col_phase, col_at = phase_of(b, (left + dj - 1) // 2)
                            total += products[
                                di * 3 + dj,
                                row_phase * 2 + col_phase,
                                :,
                                row_at : row_at + 2,
                                col_at : col_at + 4,
                                :,
                            ]
                    for mb in range(4):
                        for i in range(2):
                            for half in range(2):
                                out_ref[
                                    half,
                                    mb,
                                    4 * i + 2 * a + up,
                                    pl.ds(2 * b + left, 4, stride=4),
                                    :,
                                ] = total[mb, i, :, half * 128 : half * 128 + 128]


def decoder(latents, latent_kernel, latent_bias, gain, shift, decode_kernel, decode_bias):
    vmem = pl.BlockSpec(memory_space=pltpu.VMEM)
    out = pl.pallas_call(
        decoder_kernel,
        out_shape=jax.ShapeDtypeStruct((2, 4, 8, 16, 128), jnp.float32),
        in_specs=[vmem] * 7,
        out_specs=vmem,
        scratch_shapes=[
            pltpu.VMEM((3, 3, 2, 16, 128), jnp.float32),
            pltpu.VMEM((4, 4, 16, 64), jnp.float32),
            pltpu.VMEM((2, 256, 2048), jnp.bfloat16),
            pltpu.VMEM((4, 96, 512), jnp.float32),
            pltpu.VMEM((384, 512), jnp.bfloat16),
            pltpu.VMEM((9, 4, 4, 3, 8, 256), jnp.float32),
            pltpu.VMEM((8, 8, 128), jnp.float32),
            pltpu.VMEM((16, 8, 128), jnp.float32),
            pltpu.SemaphoreType.DMA((2, 3, 3)),
            pltpu.SemaphoreType.DMA((2, 3, 3)),
            pltpu.SemaphoreType.DMA((8,)),
            pltpu.SemaphoreType.DMA((8,)),
            pltpu.SemaphoreType.DMA((16,)),
            pltpu.SemaphoreType.DMA((16,)),
        ],
        compiler_params=pltpu.CompilerParams(
            collective_id=1, has_side_effects=True, vmem_limit_bytes=40 * 2**20
        ),
    )(
        latents,
        latent_kernel,
        latent_bias.reshape(1, 512),
        gain.reshape(1, 512),
        shift.reshape(1, 512),
        decode_kernel.reshape(9, 512, 256),
        decode_bias.reshape(1, 256),
    )
    return out.transpose(1, 2, 3, 0, 4).reshape(4, 8, 16, 256)


def shards(
    tokens,
    batch_order,
    modulation,
    expand_weight,
    expand_bias,
    reduce_weight,
    reduce_bias,
    patch_weight,
    patch_bias,
    latent_kernel,
    latent_bias,
    group_gain,
    group_shift,
    decode_kernel,
    decode_bias,
):
    col_count = lax.axis_size("col")
    row_count = lax.axis_size("row")
    col_place = lax.axis_index("col")
    section_place = lax.axis_index("section")
    tok_rows = tokens.shape[1]
    part_width = tokens.shape[2]
    full_width = part_width * col_count
    lat_rows = 2 * PR
    lat_cols = 2 * PCOLS
    rim_width = 1
    rim_edge = rim_width - 1
    expand_full, reduce_full = (
        lax.all_gather(expand_weight, "row", axis=0, tiled=True),
        lax.all_gather(reduce_weight, "row", axis=1, tiled=True),
    )

    def run_branch(normed_all):
        hidden = jnp.dot(normed_all, expand_full, preferred_element_type=jnp.float32) + expand_bias
        hidden = jax.nn.gelu(hidden, approximate=True).astype(jnp.bfloat16)
        return jnp.dot(hidden, reduce_full, preferred_element_type=jnp.float32)

    tower = []
    for section_step in range(MB):
        if True:
            chosen = batch_order[section_step]
            rows_in = lax.dynamic_index_in_dim(tokens, chosen, 0, keepdims=False)
            factors = lax.dynamic_index_in_dim(modulation, chosen, 0, keepdims=False)
            factors = lax.dynamic_slice_in_dim(factors, col_place * part_width, part_width, 1)
            row_sums, row_squares = lax.psum(
                (jnp.sum(rows_in, axis=1), jnp.sum(rows_in * rows_in, axis=1)), "col"
            )
            row_mean = (row_sums / full_width)[:, None]
            row_var = (row_squares / full_width)[:, None] - row_mean * row_mean
            normed = (
                (rows_in - row_mean) * lax.rsqrt(row_var + EPSILON) * (1.0 + factors[1])
                + factors[0]
            ).astype(jnp.bfloat16)
            tower_normed_all = lax.all_gather(normed, "col", axis=1, tiled=True)
            partial_branch = run_branch(tower_normed_all)
            branch = lax.psum_scatter(partial_branch, "col", scatter_dimension=1, tiled=True)
            residual = rows_in + factors[2] * (branch + reduce_bias)
            final_sums, final_squares = lax.psum(
                (jnp.sum(residual, axis=1), jnp.sum(residual * residual, axis=1)), "col"
            )
            final_mean = (final_sums / full_width)[:, None]
            final_var = (final_squares / full_width)[:, None] - final_mean * final_mean
            final_rows = (residual - final_mean) * lax.rsqrt(final_var + EPSILON) * (
                1.0 + factors[4]
            ) + factors[3]
            local_proj = jnp.dot(
                final_rows,
                patch_weight,
                preferred_element_type=jnp.float32,
                precision=lax.Precision.HIGHEST,
            )
            patches = lax.psum(local_proj, "col")
            patches = patches + patch_bias
            own_block = patches.reshape(PR, col_count, PCOLS, PC)
            tower.append(lax.dynamic_index_in_dim(own_block, col_place, 1, keepdims=False))
    latent = jnp.stack(tower) / 0.3611 + 0.1159
    latent = latent.reshape(MB, PR * PCOLS, LC, 4).transpose(0, 1, 3, 2).reshape(MB, PR * PCOLS, PC)
    latent = lax.dynamic_slice_in_dim(latent, 2 * section_place, 2, 0).reshape(16, PC)
    latent = jnp.pad(latent, ((0, 0), (0, 64)))
    return decoder(latent, latent_kernel, latent_bias, group_gain, group_shift, decode_kernel, decode_bias)


def solution(mesh):
    return jax.shard_map(
        shards,
        mesh=mesh,
        in_specs=(
            P(None, "row", "col"),
            P(),
            P(),
            P("row", "col"),
            P("col"),
            P("col", "row"),
            P("col"),
            P("col", None),
            P(),
            P(),
            P(),
            P(),
            P(),
            P(None, None, None, "section"),
            P("section"),
        ),
        out_specs=P(None, "row", "col", "section"),
        check_vma=False,
    )
```

time: 1020 us -> 575 us (0.56)
  the two profiles are of different devices: /device:TPU:130 before, /device:TPU:1 now
where the time goes in v1:
time: 575 us; the launch traced here: 574 us
  waiting for transfers between devices  376 us (65%)
  blocking collectives  85 us (15%)
  matrix products  54.1 us (9%)
  Pallas kernels  26 us (5%)
  between operations  21 us (4%)
  other arithmetic  8.17 us (1%)
    all_gather x1, waiting for transfers between devices, shards(): lax.all_gather(reduce_weight, 'row', axis=1, tiled=True)  146 us
    all_gather x1, waiting for transfers between devices, shards(): lax.all_gather(expand_weight, 'row', axis=0, tiled=True)  108 us
    psum x1, waiting for transfers between devices, shards(): patches = lax.psum(local_proj, 'col')  62 us
    reduce_scatter x4, waiting for transfers between devices, shards(): lax.psum_scatter(partial_branch, 'col', scatter_dimension=1, tiled=True)  58.6 us
    all_gather x4, blocking collectives, shards(): tower_normed_all = lax.all_gather(normed, 'col', axis=1, tiled=True)  55 us
    dot_general x4, matrix products, run_branch(): return jnp.dot(hidden, reduce_full, preferred_element_type=jnp.float32)  47.7 us
    pallas_call x1, Pallas kernels, decoder(): pl.pallas_call(decoder_kernel, out_shape=jax.ShapeDtypeStruct((2, 4, 8, 1...  26 us
    psum x1, blocking collectives, shards(): lax.psum((jnp.sum(rows_in, axis=1), jnp.sum(rows_in * rows_in, axis=1)),...  15 us
  transfers between devices with their start and end apart: 7, of which 5 were waited for; matrix products, arithmetic and copies ran while one was open for 7% of the time, Pallas kernels for 0%

profile of v1, /device:TPU:1, one launch (start us, length us, event | category | flops | bytes accessed | tf_op | source)
XLA Modules:
  0.0 573.9 jit_solution(11492462827678159688)
XLA Ops:
  6.5 0.7 all-gather.3.cloned.1.call-update
  7.3 0.0 all-gather.5.cloned.1.call-start
  7.3 0.7 all-gather.5.cloned.1.call-update
  8.0 0.0 reduce-scatter.9.cloned.1.call-start
  8.1 1.4 fusion.146
  16.7 1.2 dynamic-slice_reduce_fusion.3
  17.9 1.2 fusion.75
  19.2 15.0 %all-reduce.3 = (f32[64]{0:T(128)S(1)}, f32[64]{0:T(128)S(1)}, f32[64]{0:T(128)S(1)}, f32[64]{0:T(128)S(1)}, f32[64]{0:T(128)S(1)}, /*index=5*/f32[64]{0:T(128)S(1)}, f32[64]{0:T(128)S(1)}, f32[64]{0:T(128)S(1)}) all-reduce(f32[64]{0:T(128)S(1)} %get-tuple-element.12, ...), channel_id=1, replica_groups=mesh['section'=2,'row'=16,'col'=8] {'col'}, use_global_device_ids=true, to_apply=%region_33.34 | all-reduce | flops 512 | bytes 4096 | tf_op jit(solution)/shard_map/psum | solution.py:344
  34.2 1.8 fusion.124
  36.0 1.0 fusion.64
  37.0 14.4 %all_gather.22 = bf16[64,3072]{1,0:T(8,128)(2,1)S(1)} all-gather(bf16[64,384]{1,0:T(8,128)(2,1)S(1)} %fusion.64), channel_id=1, replica_groups=mesh['section'=2,'row'=16,'col'=8] {'col'}, dimensions={1}, use_global_device_ids=true | all-gather | bytes 442368 | tf_op jit(solution)/shard_map/all_gather | solution.py:353
  51.4 108.3 %all-gather.3.cloned.1.call-done = bf16[3072,1536]{1,0:T(8,128)(2,1)} async-done(((bf16[192,1536]{1,0:T(8,128)(2,1)}), bf16[3072,1536]{1,0:T(8,128)(2,1)}) %all-gather.3.cloned.1.call-update) | async-done | bytes 9437200 | tf_op jit(solution)/shard_map/all_gather | solution.py:328
  159.7 145.7 %all-gather.5.cloned.1.call-done = bf16[1536,3072]{0,1:T(8,128)(2,1)} async-done(((bf16[1536,192]{0,1:T(8,128)(2,1)}), bf16[1536,3072]{0,1:T(8,128)(2,1)}) %all-gather.5.cloned.1.call-update) | async-done | bytes 9437200 | tf_op jit(solution)/shard_map/all_gather | solution.py:329
  305.4 11.9 %fusion.26 = f32[64,3072]{1,0:T(8,128)} fusion(bf16[1536,3072]{0,1:T(8,128)(2,1)} %all-gather.5.cloned.1.call-done, bf16[64,3072]{1,0:T(8,128)(2,1)S(1)} %all_gather.22, bf16[3072,1536]{1,0:T(8,128)(2,1)} %all-gather.3.cloned.1.call-done, f32[1536]{0:T(1024)} %param.19), kind=kOutput, calls=%fused_computation.35 | convolution fusion | flops 1208942592 | bytes 20060160 | tf_op jit(solution)/shard_map/dot_general | solution.py:335
  317.3 0.0 reduce-scatter.11.cloned.1.call-start
  317.4 0.1 fusion.74
  317.5 14.3 %all_gather.23 = bf16[64,3072]{1,0:T(8,128)(2,1)S(1)} all-gather(bf16[64,384]{1,0:T(8,128)(2,1)S(1)} %get-tuple-element.76), channel_id=1, replica_groups=mesh['section'=2,'row'=16,'col'=8] {'col'}, dimensions={1}, use_global_device_ids=true | all-gather | bytes 442368 | tf_op jit(solution)/shard_map/all_gather | solution.py:353
  331.8 11.9 %fusion.35 = f32[64,3072]{1,0:T(8,128)} fusion(bf16[1536,3072]{0,1:T(8,128)(2,1)} %all-gather.5.cloned.1.call-done, bf16[64,3072]{1,0:T(8,128)(2,1)S(1)} %all_gather.23, bf16[3072,1536]{1,0:T(8,128)(2,1)} %all-gather.3.cloned.1.call-done, f32[1536]{0:T(1024)S(1)} %copy-done.8), kind=kOutput, calls=%fused_computation.44 | convolution fusion | flops 1208942592 | bytes 20060160 | tf_op jit(solution)/shard_map/dot_general | solution.py:335
  343.7 0.0 reduce-scatter.7.cloned.1.call-start
  343.8 13.1 %all_gather.21 = bf16[64,3072]{1,0:T(8,128)(2,1)S(1)} all-gather(bf16[64,384]{1,0:T(8,128)(2,1)S(1)} %get-tuple-element.75), channel_id=1, replica_groups=mesh['section'=2,'row'=16,'col'=8] {'col'}, dimensions={1}, use_global_device_ids=true | all-gather | bytes 442368 | tf_op jit(solution)/shard_map/all_gather | solution.py:353
  356.8 11.9 %fusion.17 = f32[64,3072]{1,0:T(8,128)} fusion(bf16[1536,3072]{0,1:T(8,128)(2,1)} %all-gather.5.cloned.1.call-done, bf16[64,3072]{1,0:T(8,128)(2,1)S(1)} %all_gather.21, bf16[3072,1536]{1,0:T(8,128)(2,1)} %all-gather.3.cloned.1.call-done, f32[1536]{0:T(1024)S(1)} %copy-done.8), kind=kOutput, calls=%fused_computation.26 | convolution fusion | flops 1208942592 | bytes 20060160 | tf_op jit(solution)/shard_map/dot_general | solution.py:335
  368.8 0.0 reduce-scatter.5.cloned.1.call-start
  368.8 13.3 %all_gather.18 = bf16[64,3072]{1,0:T(8,128)(2,1)S(1)} all-gather(bf16[64,384]{1,0:T(8,128)(2,1)S(1)} %get-tuple-element.74), channel_id=1, replica_groups=mesh['section'=2,'row'=16,'col'=8] {'col'}, dimensions={1}, use_global_device_ids=true | all-gather | bytes 442368 | tf_op jit(solution)/shard_map/all_gather | solution.py:353
  382.1 12.0 %fusion.8 = f32[64,3072]{1,0:T(8,128)} fusion(bf16[1536,3072]{0,1:T(8,128)(2,1)} %all-gather.5.cloned.1.call-done, bf16[64,3072]{1,0:T(8,128)(2,1)S(1)} %all_gather.18, bf16[3072,1536]{1,0:T(8,128)(2,1)} %all-gather.3.cloned.1.call-done, f32[1536]{0:T(1024)} %param.19), kind=kOutput, calls=%fused_computation.17 | convolution fusion | flops 1208942592 | bytes 20060160 | tf_op jit(solution)/shard_map/dot_general | solution.py:335
  394.2 0.0 all-reduce.6.cloned.1.call-start
  394.2 0.0 reduce-scatter.9.cloned.1.call-done
  394.3 0.0 reduce-scatter.11.cloned.1.call-done
  394.3 23.2 %reduce-scatter.7.cloned.1.call-done = f32[64,384]{1,0:T(8,128)} async-done(((f32[64,3072]{1,0:T(8,128)}), f32[64,384]{1,0:T(8,128)}) %reduce-scatter.7.cloned.1.call-update) | async-done | bytes 98320 | tf_op jit(solution)/shard_map/reduce_scatter | solution.py:355
  417.5 35.3 %reduce-scatter.5.cloned.1.call-done = f32[64,384]{1,0:T(8,128)} async-done(((f32[64,3072]{1,0:T(8,128)}), f32[64,384]{1,0:T(8,128)}) %reduce-scatter.5.cloned.1.call-update) | async-done | bytes 98320 | tf_op jit(solution)/shard_map/reduce_scatter | solution.py:355
  452.9 1.9 fusion.142
  454.8 14.9 %all-reduce.2 = (f32[64]{0:T(128)S(1)}, f32[64]{0:T(128)S(1)}, f32[64]{0:T(128)S(1)}, f32[64]{0:T(128)S(1)}, f32[64]{0:T(128)S(1)}, /*index=5*/f32[64]{0:T(128)S(1)}, f32[64]{0:T(128)S(1)}, f32[64]{0:T(128)S(1)}) all-reduce(f32[64]{0:T(128)} %get-tuple-element.71, ...), channel_id=1, replica_groups=mesh['section'=2,'row'=16,'col'=8] {'col'}, use_global_device_ids=true, to_apply=%region_38.39 | all-reduce | flops 512 | bytes 4096 | tf_op jit(solution)/shard_map/psum | solution.py:357
  469.8 1.6 fusion.91
  471.4 1.6 fusion.86
  473.0 1.6 fusion.81
  474.6 1.6 fusion.76
  476.2 62.0 %all-reduce.6.cloned.1.call-done = (f32[64,64]{1,0:T(8,128)}, f32[64,64]{1,0:T(8,128)}, f32[64,64]{1,0:T(8,128)}, f32[64,64]{1,0:T(8,128)}) async-done(((f32[64,64]{1,0:T(8,128)}, f32[64,64]{1,0:T(8,128)}, f32[64,64]{1,0:T(8,128)}, f32[64,64]{1,0:T(8,128)}), (f32[64,64]{1,0:T(8,128)}, f32[64,64]{1,0:T(8,128)}, f32[64,64]{1,0:T(8,128)}, f32[64,64]{1,0:T(8,128)})) %all-reduce.6.cloned.1.call-update) | async-done | bytes 65552 | tf_op jit(solution)/shard_map/psum | solution.py:371
  538.3 0.8 broadcast_add_fusion.3
  539.1 0.1 stack.15
  539.2 0.1 copy.31
  539.3 0.1 stack.16
  539.4 0.1 copy.32
  539.6 0.1 stack.17
  539.7 0.1 copy.33
  539.8 0.1 stack.18
  539.9 0.1 copy.34
  540.1 0.1 reshape.204
  540.2 26.0 %shard_map.145 = f32[2,4,8,16,128]{4,3,2,1,0:T(8,128)S(1)} custom-call(f32[16,128]{1,0:T(8,128)S(1)} %pad.4.lat_ref, f32[3,3,16,512]{3,2,1,0:T(8,128)S(1)} %copy-done.2, f32[1,512]{1,0:T(1,128)S(1)} %bitcast.116, f32[1,512]{1,0:T(1,128)S(1)} %bitcast.117, f32[1,512]{1,0:T(1,128)S(1)} %bitcast.118, bf16[9,512,256]{2,1,0:T(8,128)(2,1)S(1)} %bitcast.115, ...), custom_call_target="tpu_custom_call" | custom-call | tf_op jit(solution)/shard_map/pallas_call | solution.py:263
  566.2 0.9 copy_bitcast_fusion
  (38 shorter events, 0.3 us)
Async XLA Ops:
  6.5 463.3 %copy-start = (f32[384,64]{0,1:T(8,128)S(1)}, f32[384,64]{0,1:T(8,128)}, u32[]{:S(2)}) copy-start(f32[384,64]{0,1:T(8,128)} %param.22) | copy-start | bytes 294916
  6.5 153.1 %all-gather.3.cloned.1.call-start = ((), (), s32[]{:S(2)}) async-start(), calls=%async_computation.4 | async-start | bytes 10027008 | tf_op jit(solution)/shard_map/all_gather | solution.py:328
  7.3 298.1 %all-gather.5.cloned.1.call-start = ((), (), s32[]{:S(2)}) async-start(), calls=%async_computation.5 | async-start | bytes 10027008 | tf_op jit(solution)/shard_map/all_gather | solution.py:329
  8.0 386.2 %reduce-scatter.9.cloned.1.call-start = ((), (), s32[]{:S(2)}) async-start(), calls=%async_computation.8 | async-start | bytes 884736 | tf_op jit(solution)/shard_map/reduce_scatter | solution.py:355
  51.4 266.0 %copy-start.7 = (f32[4,64,384]{2,1,0:T(8,128)S(1)}, f32[4,64,384]{2,1,0:T(8,128)}, u32[]{:S(2)}) copy-start(f32[4,64,384]{2,1,0:T(8,128)} %param.15) | copy-start | bytes 1179652
  51.4 280.4 %copy-start.8 = (f32[1536]{0:T(1024)S(1)}, f32[1536]{0:T(1024)}, u32[]{:S(2)}) copy-start(f32[1536]{0:T(1024)} %param.19) | copy-start | bytes 18436
  317.3 77.0 %reduce-scatter.11.cloned.1.call-start = ((), (), s32[]{:S(2)}) async-start(), calls=%async_computation.9 | async-start | bytes 884736 | tf_op jit(solution)/shard_map/reduce_scatter | solution.py:355
  343.7 73.8 %reduce-scatter.7.cloned.1.call-start = ((), (), s32[]{:S(2)}) async-start(), calls=%async_computation.7 | async-start | bytes 884736 | tf_op jit(solution)/shard_map/reduce_scatter | solution.py:355
  368.8 84.1 %reduce-scatter.5.cloned.1.call-start = ((), (), s32[]{:S(2)}) async-start(), calls=%async_computation.6 | async-start | bytes 884736 | tf_op jit(solution)/shard_map/reduce_scatter | solution.py:355
  382.1 158.1 %copy-start.1 = (bf16[3,3,512,256]{3,2,1,0:T(8,128)(2,1)S(1)}, bf16[3,3,512,256]{3,2,1,0:T(8,128)(2,1)}, u32[]{:S(2)}) copy-start(bf16[3,3,512,256]{3,2,1,0:T(8,128)(2,1)} %param.28) | copy-start | bytes 7077892
  382.1 158.1 %copy-start.2 = (f32[3,3,16,512]{3,2,1,0:T(8,128)S(1)}, f32[3,3,16,512]{3,2,1,0:T(8,128)}, u32[]{:S(2)}) copy-start(f32[3,3,16,512]{3,2,1,0:T(8,128)} %lk_ref.1) | copy-start | bytes 884740
  382.1 158.1 %copy-start.3 = (f32[512]{0:T(512)S(1)}, f32[512]{0:T(512)}, u32[]{:S(2)}) copy-start(f32[512]{0:T(512)} %param.25) | copy-start | bytes 6148
  382.1 158.1 %copy-start.4 = (f32[512]{0:T(512)S(1)}, f32[512]{0:T(512)}, u32[]{:S(2)}) copy-start(f32[512]{0:T(512)} %param.26) | copy-start | bytes 6148
  382.1 158.1 %copy-start.5 = (f32[512]{0:T(512)S(1)}, f32[512]{0:T(512)}, u32[]{:S(2)}) copy-start(f32[512]{0:T(512)} %param.27) | copy-start | bytes 6148
  382.1 158.1 %copy-start.6 = (f32[256]{0:T(256)S(1)}, f32[256]{0:T(256)}, u32[]{:S(2)}) copy-start(f32[256]{0:T(256)} %param.29) | copy-start | bytes 3076
  394.2 144.1 %all-reduce.6.cloned.1.call-start = ((), (), s32[]{:S(2)}) async-start(), calls=%async_computation.10 | async-start | bytes 262144 | tf_op jit(solution)/shard_map/psum | solution.py:371
Sparse Core Ops, SparseCore 0:
  9.9 149.6 all-gather.2
  162.3 143.0 all-gather.4
  317.4 28.6 reduce-scatter.8
  348.7 33.7 reduce-scatter.10
  384.8 32.6 reduce-scatter.6
  420.1 32.7 reduce-scatter.4
  476.3 61.8 all-reduce.5

commit v2 on v1

--- a/solution.py
+++ b/solution.py
@@ -12,11 +12,6 @@
 N_ROW = 16
 N_COL = 8
 CELLS = 64 * 64 * 16
-LC = 16
-MB = 4
-PR = 2
-PCOLS = 4
-PC = 64
 
 
 def phase_of(base, step):
@@ -296,6 +291,442 @@
     return out.transpose(1, 2, 3, 0, 4).reshape(4, 8, 16, 256)
 
 
+WIDTH = 3072
+BLOCK = 384
+PIECE = 192
+OFFSETS = (0, -1, 1, -2, 2, -3, 3, 4)
+
+
+def tower_kernel(
+    tok_ref,
+    first_ref,
+    final_ref,
+    expand_ref,
+    reduce_ref,
+    expand_bias_ref,
+    reduce_bias_ref,
+    patch_ref,
+    patch_bias_ref,
+    out_ref,
+    normed,
+    weights,
+    total,
+    hidden,
+    based,
+    rows_in,
+    patch_all,
+    stats,
+    sib_out,
+    sib_in,
+    kept,
+    outgoing,
+    incoming,
+    residual,
+    local_sem,
+    partner_send,
+    partner_recv,
+    ring_send,
+    ring_recv,
+    stat_send,
+    stat_recv,
+    base_send,
+    base_recv,
+    patch_send,
+    patch_recv,
+    tok_send,
+    tok_recv,
+    fwd_send,
+    fwd_recv,
+    sib_send,
+    sib_recv,
+    sum_send,
+    sum_recv,
+):
+    s = lax.axis_index("section")
+    r = lax.axis_index("row")
+    c = lax.axis_index("col")
+    z, yh = r // 2, r % 2
+    x, k = c // 2, c % 2
+    quarter = 2 * yh + s
+    sibling = (s, r, 2 * x + 1 - k)
+    partner = (1 - s, 2 * z + 1 - yh, c)
+
+    def ring_place(step):
+        return (s, 2 * lax.rem(z + step + 8, 8) + yh, c)
+
+    def col_place(step):
+        return (s, r, lax.rem(c + step, 8))
+
+    def plane_place(dy, ds, dx):
+        return (lax.rem(s + ds, 2), 2 * z + lax.rem(yh + dy, 2), 2 * lax.rem(x + dx, 4) + k)
+
+    def send(source, target, send_sem, recv_sem, place):
+        copy = pltpu.make_async_remote_copy(
+            src_ref=source,
+            dst_ref=target,
+            send_sem=send_sem,
+            recv_sem=recv_sem,
+            device_id=place,
+            device_id_type=MESH,
+        )
+        copy.start()
+        return copy
+
+    sent = []
+    own_lanes = pl.ds(pl.multiple_of(quarter * BLOCK, BLOCK), BLOCK)
+    other_lanes = pl.ds(pl.multiple_of((3 - quarter) * BLOCK, BLOCK), BLOCK)
+    sources = (expand_ref, reduce_ref)
+    local = []
+    for e in range(2):
+        copy = pltpu.make_async_copy(
+            sources[e].at[:, own_lanes], weights.at[z, e, yh], local_sem.at[e]
+        )
+        copy.start()
+        local.append(copy)
+
+    barrier = pltpu.get_barrier_semaphore()
+    greet = [ring_place(1), ring_place(-1)]
+    greet += [col_place(step) for step in range(1, 8)]
+    for dy, ds in ((0, 1), (1, 0), (1, 1)):
+        greet += [plane_place(dy, ds, dx) for dx in range(4)]
+    for place in greet:
+        pl.semaphore_signal(barrier, inc=1, device_id=place, device_id_type=MESH)
+    pl.semaphore_wait(barrier, len(greet))
+
+    from_partner = []
+    for e in range(2):
+        from_partner.append(
+            send(
+                sources[e].at[:, other_lanes],
+                weights.at[z, e, yh],
+                partner_send.at[e],
+                partner_recv.at[e],
+                partner,
+            )
+        )
+    for copy in local:
+        copy.wait()
+
+    ring = {}
+    arrived = set()
+
+    def ensure(e, o, way, d):
+        if (e, o, way, d) not in arrived:
+            ring[e, o, way, d].wait_recv()
+            arrived.add((e, o, way, d))
+
+    def reach(o, way):
+        return 4 if (o == 0) == (way == 1) else 3
+
+    def ring_step(e, d, units=(0, 1)):
+        for o in units:
+            half = lax.rem(yh + o, 2)
+            for way in (1, -1):
+                if d > reach(o, way):
+                    continue
+                if d > 1:
+                    ensure(e, o, way, d - 1)
+                held = weights.at[lax.rem(z - way * (d - 1) + 8, 8), e, half]
+                index = (1 - way) // 2
+                ring[e, o, way, d] = send(
+                    held,
+                    held,
+                    ring_send.at[e, o, index, d - 1],
+                    ring_recv.at[e, o, index, d - 1],
+                    ring_place(way),
+                )
+
+    def arrive(e, d):
+        for o in range(2):
+            for way in (1, -1):
+                if d <= reach(o, way):
+                    ensure(e, o, way, d)
+
+    ring_step(0, 1, (0,))
+
+    tok = tok_ref[...].reshape(256, BLOCK)
+    lane = lax.broadcasted_iota(jnp.int32, (256, 128), 1)
+    token_sums = jnp.sum(tok, axis=1, keepdims=True)
+    token_squares = jnp.sum(tok * tok, axis=1, keepdims=True)
+    table = jnp.where(lane == 0, token_sums, jnp.where(lane == 1, token_squares, 0.0))
+    stats[c] = table.T[:8]
+    stat_copies = [
+        send(stats.at[c], stats.at[c], stat_send.at[d], stat_recv.at[d], col_place(d))
+        for d in range(1, 8)
+    ]
+    sent += stat_copies
+
+    from_partner[0].wait_recv()
+    ring_step(0, 1, (1,))
+
+    for core in range(2):
+        for group in range(8):
+            rows = pl.ds(group * 16, 16)
+            part = tok_ref[core, rows, :].reshape(2, 8, BLOCK)
+            part = part + first_ref[2, group // 4] * reduce_bias_ref[...]
+            based[core, rows, :] = part.reshape(16, BLOCK)
+
+    for copy in stat_copies:
+        copy.wait_recv()
+    table = jnp.concatenate(
+        [jnp.sum(stats[...], axis=0), jnp.zeros((120, 256), jnp.float32)], axis=0
+    ).T
+    token_mean = table[:, 0:1] * (1.0 / WIDTH)
+    token_scale = lax.rsqrt(table[:, 1:2] * (1.0 / WIDTH) - token_mean * token_mean + EPSILON)
+    plain = (tok - token_mean) * token_scale
+    for core in range(2):
+        for group in range(8):
+            start = core * 128 + group * 16
+            part = plain[start : start + 16].reshape(2, 8, BLOCK)
+            part = part * (1.0 + first_ref[1, group // 4]) + first_ref[0, group // 4]
+            normed[c, core, yh, pl.ds(group * 16, 16), :] = part.reshape(16, BLOCK).astype(
+                jnp.bfloat16
+            )
+
+    mine = normed.at[c, :, yh]
+    tok_copies = {}
+    for dy, dx in ((1, 0), (0, 1), (0, 3), (1, 1), (1, 3), (0, 2), (1, 2)):
+        tok_copies[dy, dx] = send(
+            mine, mine, tok_send.at[dy, dx], tok_recv.at[dy, dx], plane_place(dy, dy, dx)
+        )
+    tok_copies[0, 0] = send(mine, mine, tok_send.at[0, 0], tok_recv.at[0, 0], sibling)
+    sent += tok_copies.values()
+
+    base_copies = []
+    for d in range(1, 8):
+        target = lax.rem(c + d, 8)
+        rows = pl.ds(pl.multiple_of((s * 4 + target // 2) * 16, 16), 16)
+        base_copies.append(
+            send(
+                based.at[target % 2, rows, :],
+                rows_in.at[c],
+                base_send.at[d],
+                base_recv.at[d],
+                col_place(d),
+            )
+        )
+    sent += base_copies
+    own_rows = pl.ds(pl.multiple_of((s * 4 + x) * 16, 16), 16)
+    rows_in[c] = based[k, own_rows, :]
+
+    ring_step(0, 2)
+
+    forwards = []
+
+    def forward(dy, dx):
+        tok_copies[dy, dx].wait_recv()
+        piece = normed.at[2 * lax.rem(x - dx + 4, 4) + k, :, lax.rem(yh + dy, 2)]
+        forwards.append(send(piece, piece, fwd_send.at[dy, dx], fwd_recv.at[dy, dx], sibling))
+
+    for dy, dx in ((1, 0), (0, 1), (0, 3)):
+        forward(dy, dx)
+    ring_step(0, 3)
+    for dy, dx in ((1, 1), (1, 3), (0, 2), (1, 2)):
+        forward(dy, dx)
+    from_partner[1].wait_recv()
+    ring_step(1, 1)
+    sent += forwards
+
+    high = patch_ref[...].astype(jnp.bfloat16)
+    low = (patch_ref[...] - high.astype(jnp.float32)).astype(jnp.bfloat16)
+    patch_all[c] = jnp.concatenate([high, low], axis=1)
+    patch_copies = [
+        send(patch_all.at[c], patch_all.at[c], patch_send.at[d], patch_recv.at[d], col_place(d))
+        for d in range(1, 8)
+    ]
+    sent += patch_copies
+
+    tok_copies[0, 0].wait_recv()
+    for copy in forwards:
+        copy.wait_recv()
+
+    def expand(offset):
+        at = lax.rem(z + offset + 8, 8)
+        value = jnp.dot(
+            normed[at].reshape(512, BLOCK),
+            weights[at, 0].reshape(BLOCK, BLOCK),
+            preferred_element_type=jnp.float32,
+        )
+        if offset == 0:
+            total[...] = value
+        else:
+            total[...] += value
+
+    for offset in OFFSETS[:5]:
+        if offset in (-2, 2):
+            arrive(0, 2)
+        expand(offset)
+    ring_step(0, 4)
+    ring_step(1, 2)
+    arrive(0, 3)
+    expand(-3)
+    expand(3)
+    arrive(0, 4)
+    expand(4)
+    value = total[...] + expand_bias_ref[...]
+    inner = 0.7978845608028654 * (value + 0.044715 * (value * value * value))
+    value = 0.5 * value * (1.0 + jnp.tanh(inner))
+    hidden[...] = value.astype(jnp.bfloat16).reshape(2, 256, BLOCK)
+    ring_step(1, 3)
+
+    sib_copies = []
+
+    def contract(g):
+        for slot in (2 * g, 2 * g + 1):
+            at = lax.rem(z + OFFSETS[slot] + 8, 8)
+            right = weights[at, 1].reshape(BLOCK, BLOCK)
+            away = lax.dot_general(
+                hidden[1 - k], right, (((1,), (1,)), ((), ())), preferred_element_type=jnp.float32
+            )
+            sib_out[slot] = away.astype(jnp.bfloat16)
+            sib_copies.append(
+                send(
+                    sib_out.at[slot], sib_in.at[slot], sib_send.at[slot], sib_recv.at[slot], sibling
+                )
+            )
+            kept[slot] = lax.dot_general(
+                hidden[k], right, (((1,), (1,)), ((), ())), preferred_element_type=jnp.float32
+            )
+
+    m_own = yh * 8 + s * 4 + x
+    sum_copies = {}
+
+    def scatter(g):
+        for slot in (2 * g, 2 * g + 1):
+            sib_copies[slot].wait_recv()
+            value = kept[slot] + sib_in[slot].astype(jnp.float32)
+            outgoing[slot] = value.astype(jnp.bfloat16).reshape(16, 16, BLOCK)
+        pair = pl.ds(2 * g, 2)
+        for dy in range(2):
+            for ds in range(2):
+                for dx in range(4):
+                    if (dy, ds, dx) == (0, 0, 0):
+                        continue
+                    place = plane_place(dy, ds, dx)
+                    m_there = lax.rem(yh + dy, 2) * 8 + place[0] * 4 + lax.rem(x + dx, 4)
+                    m = dy * 8 + ds * 4 + dx
+                    sum_copies[g, m] = send(
+                        outgoing.at[pair, m_there],
+                        incoming.at[pair, m_own],
+                        sum_send.at[g, m],
+                        sum_recv.at[g, m],
+                        place,
+                    )
+        incoming[pair, m_own] = outgoing[pair, m_own]
+
+    contract(0)
+    ring_step(1, 4)
+    arrive(1, 2)
+    contract(1)
+    scatter(0)
+    arrive(1, 3)
+    contract(2)
+    scatter(1)
+    arrive(1, 4)
+    contract(3)
+    scatter(2)
+    scatter(3)
+
+    for copy in base_copies:
+        copy.wait_recv()
+    row_sums = jnp.zeros((2, 8, 1), jnp.float32)
+    row_squares = jnp.zeros((2, 8, 1), jnp.float32)
+    for g in range(4):
+        for m in range(1, 16):
+            sum_copies[g, m].wait_recv()
+        for slot in (2 * g, 2 * g + 1):
+            at = lax.rem(z + OFFSETS[slot] + 8, 8)
+            branch = jnp.sum(incoming[slot].astype(jnp.float32), axis=0)
+            value = rows_in[at].reshape(2, 8, BLOCK) + final_ref[0, at] * branch.reshape(
+                2, 8, BLOCK
+            )
+            residual[slot] = value
+            row_sums += jnp.sum(value, axis=2, keepdims=True)
+            row_squares += jnp.sum(value * value, axis=2, keepdims=True)
+    row_mean = row_sums * (1.0 / WIDTH)
+    row_scale = lax.rsqrt(row_squares * (1.0 / WIDTH) - row_mean * row_mean + EPSILON)
+    for copy in patch_copies:
+        copy.wait_recv()
+    projected = jnp.zeros((32, 128), jnp.float32)
+    for slot in range(8):
+        at = lax.rem(z + OFFSETS[slot] + 8, 8)
+        value = (residual[slot] - row_mean) * row_scale * (1.0 + final_ref[2, at]) + final_ref[
+            1, at
+        ]
+        value = value.reshape(16, BLOCK)
+        high = value.astype(jnp.bfloat16)
+        low = (value - high.astype(jnp.float32)).astype(jnp.bfloat16)
+        projected += jnp.dot(
+            jnp.concatenate([high, low], axis=0),
+            patch_all[at],
+            preferred_element_type=jnp.float32,
+        )
+    patch = projected[:16, :64] + (projected[16:, :64] + projected[:16, 64:])
+    latent = (patch + patch_bias_ref[...]) / 0.3611 + 0.1159
+    out_ref[...] = jnp.concatenate([latent, jnp.zeros((16, 64), jnp.float32)], axis=1)
+
+    for copy in from_partner:
+        copy.wait_send()
+    for copy in ring.values():
+        copy.wait_send()
+    for copy in sent:
+        copy.wait_send()
+    for copy in sib_copies:
+        copy.wait_send()
+    for copy in sum_copies.values():
+        copy.wait_send()
+
+
+def tower(tok, first, final, expand, reduce_t, expand_bias, reduce_bias, patch, patch_bias):
+    vmem = pl.BlockSpec(memory_space=pltpu.VMEM)
+    bf16, f32 = jnp.bfloat16, jnp.float32
+    dma = pltpu.SemaphoreType.DMA
+    return pl.pallas_call(
+        tower_kernel,
+        out_shape=jax.ShapeDtypeStruct((16, 128), f32),
+        in_specs=[vmem] * 9,
+        out_specs=vmem,
+        scratch_shapes=[
+            pltpu.VMEM((8, 2, 2, 128, BLOCK), bf16),
+            pltpu.VMEM((8, 2, 2, PIECE, BLOCK), bf16),
+            pltpu.VMEM((512, BLOCK), f32),
+            pltpu.VMEM((2, 256, BLOCK), bf16),
+            pltpu.VMEM((2, 128, BLOCK), f32),
+            pltpu.VMEM((8, 16, BLOCK), f32),
+            pltpu.VMEM((8, BLOCK, 128), bf16),
+            pltpu.VMEM((8, 8, 256), f32),
+            pltpu.VMEM((8, 256, BLOCK), bf16),
+            pltpu.VMEM((8, 256, BLOCK), bf16),
+            pltpu.VMEM((8, 256, BLOCK), f32),
+            pltpu.VMEM((8, 16, 16, BLOCK), bf16),
+            pltpu.VMEM((8, 16, 16, BLOCK), bf16),
+            pltpu.VMEM((8, 2, 8, BLOCK), f32),
+            dma((2,)),
+            dma((2,)),
+            dma((2,)),
+            dma((2, 2, 2, 4)),
+            dma((2, 2, 2, 4)),
+            dma((8,)),
+            dma((8,)),
+            dma((8,)),
+            dma((8,)),
+            dma((8,)),
+            dma((8,)),
+            dma((2, 4)),
+            dma((2, 4)),
+            dma((2, 4)),
+            dma((2, 4)),
+            dma((8,)),
+            dma((8,)),
+            dma((4, 16)),
+            dma((4, 16)),
+        ],
+        compiler_params=pltpu.CompilerParams(
+            collective_id=0, has_side_effects=True, vmem_limit_bytes=48 * 2**20
+        ),
+    )(tok, first, final, expand, reduce_t, expand_bias, reduce_bias, patch, patch_bias)
+
+
 def shards(
     tokens,
     batch_order,
@@ -313,70 +744,32 @@
     decode_kernel,
     decode_bias,
 ):
-    col_count = lax.axis_size("col")
-    row_count = lax.axis_size("row")
-    col_place = lax.axis_index("col")
-    section_place = lax.axis_index("section")
-    tok_rows = tokens.shape[1]
-    part_width = tokens.shape[2]
-    full_width = part_width * col_count
-    lat_rows = 2 * PR
-    lat_cols = 2 * PCOLS
-    rim_width = 1
-    rim_edge = rim_width - 1
-    expand_full, reduce_full = (
-        lax.all_gather(expand_weight, "row", axis=0, tiled=True),
-        lax.all_gather(reduce_weight, "row", axis=1, tiled=True),
+    s = lax.axis_index("section")
+    r = lax.axis_index("row")
+    c = lax.axis_index("col")
+    quarter = 2 * (r % 2) + s
+    tok = jnp.take(tokens, batch_order, axis=0)
+    tok = tok.reshape(2, 2, 2, 4, 2, 4, BLOCK).transpose(4, 0, 3, 1, 2, 5, 6).reshape(2, 128, BLOCK)
+    factors = jnp.take(modulation, batch_order, axis=0)
+    first = lax.dynamic_slice_in_dim(factors, c * BLOCK, BLOCK, 2)[:, :3]
+    first = first.transpose(1, 0, 2).reshape(3, 2, 2, 1, BLOCK)
+    final = lax.dynamic_slice_in_dim(factors, 2 * s, 2, 0)[:, 2:]
+    final = final.reshape(2, 3, 8, 1, BLOCK).transpose(1, 2, 0, 3, 4)
+    patch = patch_weight.reshape(BLOCK, 16, 4).transpose(0, 2, 1).reshape(BLOCK, 64)
+    latents = tower(
+        tok,
+        first,
+        final,
+        expand_weight,
+        reduce_weight.T,
+        lax.dynamic_slice_in_dim(expand_bias, quarter * BLOCK, BLOCK, 0).reshape(1, BLOCK),
+        reduce_bias.reshape(1, BLOCK),
+        patch,
+        patch_bias.reshape(16, 4).T.reshape(1, 64),
     )
-
-    def run_branch(normed_all):
-        hidden = jnp.dot(normed_all, expand_full, preferred_element_type=jnp.float32) + expand_bias
-        hidden = jax.nn.gelu(hidden, approximate=True).astype(jnp.bfloat16)
-        return jnp.dot(hidden, reduce_full, preferred_element_type=jnp.float32)
-
-    tower = []
-    for section_step in range(MB):
-        if True:
-            chosen = batch_order[section_step]
-            rows_in = lax.dynamic_index_in_dim(tokens, chosen, 0, keepdims=False)
-            factors = lax.dynamic_index_in_dim(modulation, chosen, 0, keepdims=False)
-            factors = lax.dynamic_slice_in_dim(factors, col_place * part_width, part_width, 1)
-            row_sums, row_squares = lax.psum(
-                (jnp.sum(rows_in, axis=1), jnp.sum(rows_in * rows_in, axis=1)), "col"
-            )
-            row_mean = (row_sums / full_width)[:, None]
-            row_var = (row_squares / full_width)[:, None] - row_mean * row_mean
-            normed = (
-                (rows_in - row_mean) * lax.rsqrt(row_var + EPSILON) * (1.0 + factors[1])
-                + factors[0]
-            ).astype(jnp.bfloat16)
-            tower_normed_all = lax.all_gather(normed, "col", axis=1, tiled=True)
-            partial_branch = run_branch(tower_normed_all)
-            branch = lax.psum_scatter(partial_branch, "col", scatter_dimension=1, tiled=True)
-            residual = rows_in + factors[2] * (branch + reduce_bias)
-            final_sums, final_squares = lax.psum(
-                (jnp.sum(residual, axis=1), jnp.sum(residual * residual, axis=1)), "col"
-            )
-            final_mean = (final_sums / full_width)[:, None]
-            final_var = (final_squares / full_width)[:, None] - final_mean * final_mean
-            final_rows = (residual - final_mean) * lax.rsqrt(final_var + EPSILON) * (
-                1.0 + factors[4]
-            ) + factors[3]
-            local_proj = jnp.dot(
-                final_rows,
-                patch_weight,
-                preferred_element_type=jnp.float32,
-                precision=lax.Precision.HIGHEST,
-            )
-            patches = lax.psum(local_proj, "col")
-            patches = patches + patch_bias
-            own_block = patches.reshape(PR, col_count, PCOLS, PC)
-            tower.append(lax.dynamic_index_in_dim(own_block, col_place, 1, keepdims=False))
-    latent = jnp.stack(tower) / 0.3611 + 0.1159
-    latent = latent.reshape(MB, PR * PCOLS, LC, 4).transpose(0, 1, 3, 2).reshape(MB, PR * PCOLS, PC)
-    latent = lax.dynamic_slice_in_dim(latent, 2 * section_place, 2, 0).reshape(16, PC)
-    latent = jnp.pad(latent, ((0, 0), (0, 64)))
-    return decoder(latent, latent_kernel, latent_bias, group_gain, group_shift, decode_kernel, decode_bias)
+    return decoder(
+        latents, latent_kernel, latent_bias, group_gain, group_shift, decode_kernel, decode_bias
+    )
 
 
 def solution(mesh):

time: 575 us -> 123 us (0.21)
  waiting for transfers between devices: 376 us -> 0 us
  blocking collectives: 85 us -> 0 us
  Pallas kernels: 26 us -> 108 us
  matrix products: 54.1 us -> 0 us
  between operations: 21 us -> 0.21 us
  local copies, waits for them, and re-layouts: 3.29 us -> 12.6 us
  other arithmetic: 8.17 us -> 1.69 us
    all_gather x2 -> x0, waiting for transfers between devices: 254 us -> none  [the longest x1 146 us: shards(): lax.all_gather(reduce_weight, 'row', axis=1, tiled=True)]
    pallas_call x0 -> x1, Pallas kernels: none -> 84.1 us  [tower(): pl.pallas_call(tower_kernel, out_shape=jax.ShapeDtypeStruct((16, 128), f3...]
    psum x1 -> x0, waiting for transfers between devices: 62 us -> none  [shards(): patches = lax.psum(local_proj, 'col')]
    reduce_scatter x4 -> x0, waiting for transfers between devices: 58.6 us -> none  [shards(): lax.psum_scatter(partial_branch, 'col', scatter_dimension=1, tiled=True)]
    all_gather x4 -> x0, blocking collectives: 55 us -> none  [shards(): tower_normed_all = lax.all_gather(normed, 'col', axis=1, tiled=True)]
    dot_general x8 -> x0, matrix products: 54.1 us -> none  [the longest x4 47.7 us: run_branch(): return jnp.dot(hidden, reduce_full, preferred_element_type=jnp.float32)]
    psum x2 -> x0, blocking collectives: 30 us -> none  [the longest x1 15 us: shards(): lax.psum((jnp.sum(rows_in, axis=1), jnp.sum(rows_in * rows_in, axis=1)),...]
  transfers between devices with their start and end apart: 7 -> 0, of which waited for: 5 -> 0; matrix products, arithmetic and copies ran while one was open for 7% -> 0% of each run, Pallas kernels for 0% -> 0%
where the time goes in v2:
time: 123 us
  Pallas kernels  108 us (88%)
  local copies, waits for them, and re-layouts  12.6 us (10%)
  other arithmetic  1.69 us (1%)
    pallas_call x1, Pallas kernels, tower(): pl.pallas_call(tower_kernel, out_shape=jax.ShapeDtypeStruct((16, 128), f3...  84.1 us
    pallas_call x1, Pallas kernels, decoder(): pl.pallas_call(decoder_kernel, out_shape=jax.ShapeDtypeStruct((2, 4, 8, 1...  24.3 us
    unnamed x22, local copies, waits for them, and re-layouts  3.12 us
    gather x2, local copies, waits for them, and re-layouts, shards(): tok = jnp.take(tokens, batch_order, axis=0)  2.58 us

profile of v2, /device:TPU:1, one launch (start us, length us, event | category | flops | bytes accessed | tf_op | source)
XLA Modules:
  0.0 122.9 jit_solution(4773479261840624502)
XLA Ops:
  0.0 0.0 copy-start
  0.0 0.0 copy-start.10
  0.0 0.8 dynamic_slice.11
  0.8 0.7 compare_select_fusion
  1.5 2.1 %gather_fusion.1 = f32[4,5,3072]{2,0,1:T(4,128)S(1)} fusion(f32[4,5,3072]{2,0,1:T(4,128)} %param.17, s32[1024]{0:T(1024)S(1)} %pad_clamp_fusion), kind=kCustom, calls=%fused_computation.1 | custom fusion | bytes 491536 | tf_op jit(solution)/shard_map/jit(_take)/gather | solution.py:753
  3.6 0.0 copy-done.10
  3.6 0.0 copy-start.9
  3.6 0.1 broadcast_select_fusion
  3.8 0.1 reshape.56
  3.9 0.1 copy.36
  4.0 0.0 copy-done
  4.0 1.3 %gather_fusion = f32[4,64,384]{2,1,0:T(8,128)} fusion(f32[4,64,384]{2,1,0:T(8,128)S(1)} %copy-done, s32[1024]{0:T(1024)S(1)} %pad_clamp_fusion), kind=kCustom, calls=%fused_computation | custom fusion | bytes 786448 | tf_op jit(solution)/shard_map/jit(_take)/gather | solution.py:751
  5.3 0.0 copy-start.1
  5.3 0.0 copy-start.5
  5.3 0.0 copy-start.6
  5.3 0.0 copy-start.7
  5.3 0.0 copy-start.8
  5.3 1.3 %gather.11 = f32[2,2,2,4,2,4,384]{6,5,4,3,2,1,0:T(4,128)S(1)} reshape(f32[4,64,384]{2,1,0:T(8,128)} %gather_fusion) | data formatting | bytes 786432 | tf_op jit(solution)/shard_map/jit(_take)/gather | solution.py:751
  6.6 0.1 broadcast_in_dim.24
  6.7 0.9 fusion
  7.6 1.1 reshape.54.tok_ref
  8.7 0.0 copy-done.9
  8.8 0.1 copy.28.patch_ref
  8.9 0.7 reshape.61
  9.7 0.1 copy.27
  9.7 0.1 reshape.62.patch_bias_ref
  9.8 0.7 reshape.58.reduce_bias_ref
  10.5 0.0 copy-start.2
  10.5 1.1 copy-done.2
  11.6 0.0 copy-start.3
  11.6 1.1 copy-done.3
  12.7 84.1 %shard_map.145.lat_ref = f32[16,128]{1,0:T(8,128)S(1)} custom-call(f32[2,128,384]{2,1,0:T(8,128)S(1)} %reshape.54.tok_ref, f32[3,2,2,1,384]{4,3,2,1,0:T(1,128)S(1)} %reshape.55.first_ref, f32[3,8,2,1,384]{4,3,2,1,0:T(1,128)S(1)} %bitcast.28, bf16[192,1536]{1,0:T(8,128)(2,1)S(1)} %copy-done.2, bf16[192,1536]{1,0:T(8,128)(2,1)S(1)} %bitcast.27, ...), custom_call_target="tpu_custom_call" | custom-call | tf_op jit(solution)/shard_map/pallas_call | solution.py:684
  96.8 0.0 copy-done.1
  96.8 0.0 copy-done.5
  96.8 0.0 copy-done.6
  96.8 0.0 copy-done.7
  96.8 0.0 copy-done.8
  96.8 0.0 copy-start.4
  96.8 1.0 copy-done.4
  97.8 24.3 %shard_map.146 = f32[2,4,8,16,128]{4,3,2,1,0:T(8,128)S(1)} custom-call(f32[16,128]{1,0:T(8,128)S(1)} %shard_map.145.lat_ref, f32[3,3,16,512]{3,2,1,0:T(8,128)S(1)} %copy-done.4, f32[1,512]{1,0:T(1,128)S(1)} %bitcast.29, f32[1,512]{1,0:T(1,128)S(1)} %bitcast.30, f32[1,512]{1,0:T(1,128)S(1)} %bitcast.31, bf16[9,512,256]{2,1,0:T(8,128)(2,1)S(1)} %bitcast.26, ...), custom_call_target="tpu_custom_call" | custom-call | tf_op jit(solution)/shard_map/pallas_call | solution.py:258
  122.1 0.9 copy_bitcast_fusion
  (8 shorter events, 0.1 us)
Async XLA Ops:
  0.0 4.0 %copy-start = (f32[4,64,384]{2,1,0:T(8,128)S(1)}, f32[4,64,384]{2,1,0:T(8,128)}, u32[]{:S(2)}) copy-start(f32[4,64,384]{2,1,0:T(8,128)} %param.15) | copy-start | bytes 1179652
  0.0 3.6 %copy-start.10 = (s32[4]{0:T(128)S(1)}, s32[4]{0:T(128)}, u32[]{:S(2)}) copy-start(s32[4]{0:T(128)} %param.16) | copy-start | bytes 52
  3.6 5.1 %copy-start.9 = (f32[384,64]{0,1:T(8,128)S(1)}, f32[384,64]{0,1:T(8,128)}, u32[]{:S(2)}) copy-start(f32[384,64]{0,1:T(8,128)} %param.22) | copy-start | bytes 294916
  5.3 91.5 %copy-start.1 = (bf16[3,3,512,256]{3,2,1,0:T(8,128)(2,1)S(1)}, bf16[3,3,512,256]{3,2,1,0:T(8,128)(2,1)}, u32[]{:S(2)}) copy-start(bf16[3,3,512,256]{3,2,1,0:T(8,128)(2,1)} %param.28) | copy-start | bytes 7077892
  5.3 91.5 %copy-start.5 = (f32[512]{0:T(512)S(1)}, f32[512]{0:T(512)}, u32[]{:S(2)}) copy-start(f32[512]{0:T(512)} %param.25) | copy-start | bytes 6148
  5.3 91.5 %copy-start.6 = (f32[512]{0:T(512)S(1)}, f32[512]{0:T(512)}, u32[]{:S(2)}) copy-start(f32[512]{0:T(512)} %param.26) | copy-start | bytes 6148
  5.3 91.5 %copy-start.7 = (f32[512]{0:T(512)S(1)}, f32[512]{0:T(512)}, u32[]{:S(2)}) copy-start(f32[512]{0:T(512)} %param.27) | copy-start | bytes 6148
  5.3 91.5 %copy-start.8 = (f32[256]{0:T(256)S(1)}, f32[256]{0:T(256)}, u32[]{:S(2)}) copy-start(f32[256]{0:T(256)} %param.29) | copy-start | bytes 3076
  10.5 1.1 copy-start.2
  11.6 1.1 copy-start.3
  96.8 1.0 copy-start.4

commit v3 on v1

v3 whole, which is shorter than its diff:
```python
from types import SimpleNamespace

import jax
import jax.numpy as jnp
from jax import lax
from jax.experimental import pallas as pl
from jax.experimental.pallas import tpu as pltpu
from jax.sharding import PartitionSpec as P

MESH = pl.DeviceIdType.MESH
EPSILON = 1e-06
N_ROW = 16
N_COL = 8
CELLS = 64 * 64 * 16
WIDTH = 3072
BLOCK = 384
PIECE = 192
GROUPS = ((0, -1, 1), (-2, 2), (-3, 3), (4,))
OFFSETS = (0, -1, 1, -2, 2, -3, 3, 4)
BF16, F32 = jnp.bfloat16, jnp.float32
DMA = pltpu.SemaphoreType.DMA
INPUTS = {
    "tokens": pl.ANY,
    "order": pltpu.SMEM,
    "modulation": pl.ANY,
    "expand": pl.ANY,
    "expand_bias": pltpu.VMEM,
    "reduce": pl.ANY,
    "reduce_bias": pltpu.VMEM,
    "patch": pltpu.VMEM,
    "patch_bias": pltpu.VMEM,
    "latent_kernel": pl.ANY,
    "latent_bias": pltpu.VMEM,
    "gain": pltpu.VMEM,
    "shift": pltpu.VMEM,
    "decode_kernel": pl.ANY,
    "decode_bias": pltpu.VMEM,
}
SCRATCH = {
    "tokens_in": pltpu.VMEM((4, 64, BLOCK), F32),
    "factors": pltpu.VMEM((5, 4, WIDTH), F32),
    "latent_in": pltpu.VMEM((3, 3, 16, 512), F32),
    "decode_in": pltpu.VMEM((9, 512, 256), BF16),
    "tok": pltpu.VMEM((2, 128, BLOCK), F32),
    "first": pltpu.VMEM((3, 2, 2, 1, BLOCK), F32),
    "final": pltpu.VMEM((3, 8, 2, 1, BLOCK), F32),
    "normed": pltpu.VMEM((8, 2, 2, 128, BLOCK), BF16),
    "weights": pltpu.VMEM((8, 2, 2, PIECE, BLOCK), BF16),
    "total": pltpu.VMEM((512, BLOCK), F32),
    "hidden": pltpu.VMEM((2, 256, BLOCK), BF16),
    "based": pltpu.VMEM((2, 128, BLOCK), F32),
    "rows_in": pltpu.VMEM((8, 16, BLOCK), F32),
    "patch_all": pltpu.VMEM((8, BLOCK, 128), BF16),
    "stats": pltpu.VMEM((8, 8, 256), F32),
    "sib_out": pltpu.VMEM((8, 256, BLOCK), BF16),
    "sib_in": pltpu.VMEM((8, 256, BLOCK), BF16),
    "kept": pltpu.VMEM((8, 256, BLOCK), F32),
    "outgoing": pltpu.VMEM((8, 16, 16, BLOCK), BF16),
    "incoming": pltpu.VMEM((8, 16, 16, BLOCK), BF16),
    "residual": pltpu.VMEM((8, 2, 8, BLOCK), F32),
    "latents": pltpu.VMEM((16, 128), F32),
    "blocks": pltpu.VMEM((3, 3, 2, 16, 128), F32),
    "patches": pltpu.VMEM((4, 4, 16, 64), F32),
    "taps": pltpu.VMEM((2, 256, 2048), BF16),
    "act": pltpu.VMEM((4, 96, 512), F32),
    "cells": pltpu.VMEM((384, 512), BF16),
    "products": pltpu.VMEM((9, 4, 4, 3, 8, 256), F32),
    "col_stats": pltpu.VMEM((8, 8, 128), F32),
    "row_stats": pltpu.VMEM((16, 8, 128), F32),
    "load_sem": DMA((8,)),
    "partner_send": DMA((2,)),
    "partner_recv": DMA((2,)),
    "ring_send": DMA((2, 2, 2, 4)),
    "ring_recv": DMA((2, 2, 2, 4)),
    "stat_send": DMA((8,)),
    "stat_recv": DMA((8,)),
    "base_send": DMA((8,)),
    "base_recv": DMA((8,)),
    "patch_send": DMA((8,)),
    "patch_recv": DMA((8,)),
    "tok_send": DMA((2, 4)),
    "tok_recv": DMA((2, 4)),
    "fwd_send": DMA((2, 4)),
    "fwd_recv": DMA((2, 4)),
    "sib_send": DMA((8,)),
    "sib_recv": DMA((8,)),
    "sum_send": DMA((4, 16)),
    "sum_recv": DMA((4, 16)),
    "halo_send": DMA((2, 3, 3)),
    "halo_recv": DMA((2, 3, 3)),
    "col_send": DMA((8,)),
    "col_recv": DMA((8,)),
    "row_send": DMA((16,)),
    "row_recv": DMA((16,)),
}


def phase_of(base, step):
    if base == 0:
        return [(1, 0), (0, 0), (1, 1)][step + 1]
    return [(0, 0), (1, 1), (0, 1)][step + 1]


def program_kernel(*refs):
    names = [*INPUTS, "out", *SCRATCH]
    m = SimpleNamespace(**dict(zip(names, refs, strict=True)))
    s = lax.axis_index("section")
    r = lax.axis_index("row")
    c = lax.axis_index("col")
    z, yh = r // 2, r % 2
    x, k = c // 2, c % 2
    quarter = 2 * yh + s
    sibling = (s, r, 2 * x + 1 - k)
    partner = (1 - s, 2 * z + 1 - yh, c)

    def ring_place(step):
        return (s, 2 * lax.rem(z + step + 8, 8) + yh, c)

    def col_place(step):
        return (s, r, lax.rem(c + step, 8))

    def plane_place(dy, ds, dx):
        return (lax.rem(s + ds, 2), 2 * z + lax.rem(yh + dy, 2), 2 * lax.rem(x + dx, 4) + k)

    def send(source, target, send_sem, recv_sem, place):
        copy = pltpu.make_async_remote_copy(
            src_ref=source,
            dst_ref=target,
            send_sem=send_sem,
            recv_sem=recv_sem,
            device_id=place,
            device_id_type=MESH,
        )
        copy.start()
        return copy

    sent = []

    def place(ds, dr, dc):
        return (
            lax.rem(s + ds, 2),
            lax.rem(r + dr + N_ROW, N_ROW),
            lax.rem(c + dc + N_COL, N_COL),
        )

    def load(source, target, index):
        copy = pltpu.make_async_copy(source, target, m.load_sem.at[index])
        copy.start()
        return copy

    own_cols = pl.ds(pl.multiple_of(quarter * BLOCK, BLOCK), BLOCK)
    other_cols = pl.ds(pl.multiple_of((3 - quarter) * BLOCK, BLOCK), BLOCK)
    load_expand = load(m.expand.at[:, own_cols], m.weights.at[z, 0, yh], 0)
    load_tokens = load(m.tokens, m.tokens_in, 1)
    load_factors = load(m.modulation, m.factors, 2)
    load_reduce = [
        load(m.reduce.at[:, own_cols], m.weights.at[z, 1, yh], 3),
    ]
    load_latent = load(m.latent_kernel, m.latent_in, 5)
    load_decode = load(m.decode_kernel, m.decode_in, 6)

    halo = []
    for ds in range(2):
        for dr in (-1, 0, 1):
            for dc in (-1, 0, 1):
                if (ds, dr, dc) != (0, 0, 0):
                    halo.append((ds, dr, dc))

    barrier = pltpu.get_barrier_semaphore()
    greet = [place(0, step, 0) for step in range(1, N_ROW)]
    greet += [col_place(step) for step in range(1, N_COL)]
    for dy, ds in ((0, 1), (1, 0), (1, 1)):
        greet += [plane_place(dy, ds, dx) for dx in range(4)]
    greet += [place(*h) for h in halo if h[0] * (h[1] or h[2]) or h[1] * h[2]]
    for target in greet:
        pl.semaphore_signal(barrier, inc=1, device_id=target, device_id_type=MESH)
    pl.semaphore_wait(barrier, len(greet))

    def to_partner(e, source):
        return send(
            source, m.weights.at[z, e, yh], m.partner_send.at[e], m.partner_recv.at[e], partner
        )

    from_partner = [to_partner(0, m.expand.at[:, other_cols])]
    ring = {}
    arrived = set()

    def ensure(e, o, way, d):
        if (e, o, way, d) not in arrived:
            ring[e, o, way, d].wait_recv()
            arrived.add((e, o, way, d))

    def reach(o, way):
        return 4 if (o == 0) == (way == 1) else 3

    def ring_step(e, d, units=(0, 1)):
        for o in units:
            half = lax.rem(yh + o, 2)
            for way in (1, -1):
                if d > reach(o, way):
                    continue
                if d > 1:
                    ensure(e, o, way, d - 1)
                held = m.weights.at[lax.rem(z - way * (d - 1) + 8, 8), e, half]
                index = (1 - way) // 2
                ring[e, o, way, d] = send(
                    held,
                    held,
                    m.ring_send.at[e, o, index, d - 1],
                    m.ring_recv.at[e, o, index, d - 1],
                    ring_place(way),
                )

    def arrive(e, d):
        for o in range(2):
            for way in (1, -1):
                if d <= reach(o, way):
                    ensure(e, o, way, d)

    load_expand.wait()
    ring_step(0, 1, (0,))

    load_tokens.wait()
    for slot in range(4):
        rows = m.tokens_in[m.order[slot]]
        for col in range(8):
            start = (slot // 2 * 4 + col // 2) * 16 + slot % 2 * 8
            m.tok[col % 2, start : start + 8, :] = jnp.concatenate(
                [rows[col * 4 : col * 4 + 4], rows[32 + col * 4 : 36 + col * 4]], axis=0
            )
    tok = m.tok[...].reshape(256, BLOCK)
    lane = lax.broadcasted_iota(jnp.int32, (256, 128), 1)
    token_sums = jnp.sum(tok, axis=1, keepdims=True)
    token_squares = jnp.sum(tok * tok, axis=1, keepdims=True)
    table = jnp.where(lane == 0, token_sums, jnp.where(lane == 1, token_squares, 0.0))
    m.stats[c] = table.T[:8]
    stat_copies = [
        send(m.stats.at[c], m.stats.at[c], m.stat_send.at[d], m.stat_recv.at[d], col_place(d))
        for d in range(1, 8)
    ]
    sent += stat_copies

    from_partner[0].wait_recv()
    ring_step(0, 1, (1,))

    load_factors.wait()
    lanes = pl.ds(pl.multiple_of(c * BLOCK, BLOCK), BLOCK)
    for slot in range(4):
        for j in range(3):
            m.first[j, slot // 2, slot % 2] = m.factors[j, pl.ds(m.order[slot], 1), lanes]

    for copy in stat_copies:
        copy.wait_recv()
    table = jnp.concatenate([jnp.sum(m.stats[...], axis=0), jnp.zeros((120, 256), F32)], axis=0).T
    token_mean = table[:, 0:1] * (1.0 / WIDTH)
    token_scale = lax.rsqrt(table[:, 1:2] * (1.0 / WIDTH) - token_mean * token_mean + EPSILON)
    plain = (tok - token_mean) * token_scale
    for core in range(2):
        for group in range(8):
            start = core * 128 + group * 16
            part = plain[start : start + 16].reshape(2, 8, BLOCK)
            part = part * (1.0 + m.first[1, group // 4]) + m.first[0, group // 4]
            m.normed[c, core, yh, pl.ds(group * 16, 16), :] = part.reshape(16, BLOCK).astype(BF16)

    mine = m.normed.at[c, :, yh]
    tok_copies = {}
    for dy, dx in ((1, 0), (0, 1), (0, 3), (1, 1), (1, 3), (0, 2), (1, 2)):
        tok_copies[dy, dx] = send(
            mine, mine, m.tok_send.at[dy, dx], m.tok_recv.at[dy, dx], plane_place(dy, dy, dx)
        )
    tok_copies[0, 0] = send(mine, mine, m.tok_send.at[0, 0], m.tok_recv.at[0, 0], sibling)
    sent += tok_copies.values()

    ring_step(0, 2)

    for copy in load_reduce:
        copy.wait()
    from_partner.append(to_partner(1, m.reduce.at[:, other_cols]))

    for core in range(2):
        for group in range(8):
            rows = pl.ds(group * 16, 16)
            part = m.tok[core, rows, :].reshape(2, 8, BLOCK)
            part = part + m.first[2, group // 4] * m.reduce_bias[...].reshape(1, BLOCK)
            m.based[core, rows, :] = part.reshape(16, BLOCK)
    base_copies = []
    for d in range(1, 8):
        target = lax.rem(c + d, 8)
        rows = pl.ds(pl.multiple_of((s * 4 + target // 2) * 16, 16), 16)
        base_copies.append(
            send(
                m.based.at[target % 2, rows, :],
                m.rows_in.at[c],
                m.base_send.at[d],
                m.base_recv.at[d],
                col_place(d),
            )
        )
    sent += base_copies
    own_rows = pl.ds(pl.multiple_of((s * 4 + x) * 16, 16), 16)
    m.rows_in[c] = m.based[k, own_rows, :]

    forwards = []

    def forward(dy, dx):
        tok_copies[dy, dx].wait_recv()
        piece = m.normed.at[2 * lax.rem(x - dx + 4, 4) + k, :, lax.rem(yh + dy, 2)]
        forwards.append(send(piece, piece, m.fwd_send.at[dy, dx], m.fwd_recv.at[dy, dx], sibling))

    forward(1, 0)
    ring_step(0, 3)
    for dy, dx in ((0, 1), (0, 3)):
        forward(dy, dx)

    source = lax.broadcasted_iota(jnp.int32, (64, 64), 0)
    target = lax.broadcasted_iota(jnp.int32, (64, 64), 1)
    swap = target == source % 4 * 16 + source // 4
    swap_bf16 = (source == target % 4 * 16 + target // 4).astype(F32).astype(BF16)
    patch_high = m.patch[...].astype(BF16)
    patch_low = (m.patch[...] - patch_high.astype(F32)).astype(BF16)
    m.patch_all[c] = jnp.concatenate(
        [jnp.dot(swap_bf16, part, preferred_element_type=F32) for part in (patch_high, patch_low)],
        axis=0,
    ).T.astype(BF16)
    patch_bias = jnp.dot(
        jnp.zeros((8, 64), F32) + m.patch_bias[...].reshape(1, 64),
        swap.astype(F32),
        preferred_element_type=F32,
        precision=lax.Precision.HIGHEST,
    )[:1]
    load_latent.wait()
    m.taps[...] = jnp.zeros_like(m.taps)
    for u in range(2):
        for v in range(2):
            for sa in range(2):
                for sb in range(2):
                    for a in range(2):
                        for b in range(2):
                            di = 2 * u + sa - 2 + a
                            dj = 2 * v + sb - 2 + b
                            if abs(di) <= 1 and abs(dj) <= 1:
                                row = ((u * 2 + v) * 2 + sa) * 2 + sb
                                tap = m.latent_in[di + 1, dj + 1]
                                high = tap.astype(jnp.bfloat16)
                                low = (tap - high.astype(jnp.float32)).astype(jnp.bfloat16)
                                phase = 2 * a + b
                                rows = pl.ds(row * 16, 16)
                                lanes = pl.ds(phase * 512, 512)
                                m.taps[0, rows, lanes] = high
                                m.taps[1, rows, lanes] = low
    m.patches[...] = jnp.zeros_like(m.patches)

    for slot in range(2):
        for j in range(3):
            for at in range(8):
                m.final[j, at, slot] = m.factors[
                    j + 2, pl.ds(m.order[2 * s + slot], 1), at * BLOCK : (at + 1) * BLOCK
                ]

    ring_step(1, 1, (0,))
    for dy, dx in ((1, 1), (1, 3)):
        forward(dy, dx)
    ring_step(0, 4)
    from_partner[1].wait_recv()
    ring_step(1, 1, (1,))
    for dy, dx in ((0, 2), (1, 2)):
        forward(dy, dx)
    sent += forwards

    patch_copies = [
        send(
            m.patch_all.at[c],
            m.patch_all.at[c],
            m.patch_send.at[d],
            m.patch_recv.at[d],
            col_place(d),
        )
        for d in range(1, 8)
    ]
    sent += patch_copies

    tok_copies[0, 0].wait_recv()
    for copy in forwards:
        copy.wait_recv()

    def expand(offset):
        at = lax.rem(z + offset + 8, 8)
        value = jnp.dot(
            m.normed[at].reshape(512, BLOCK),
            m.weights[at, 0].reshape(BLOCK, BLOCK),
            preferred_element_type=F32,
        )
        if offset == 0:
            m.total[...] = value
        else:
            m.total[...] += value

    arrive(0, 2)
    for offset in OFFSETS[:5]:
        expand(offset)
    ring_step(1, 2)
    arrive(0, 3)
    expand(-3)
    expand(3)
    arrive(0, 4)
    expand(4)
    value = m.total[...] + m.expand_bias[own_cols].reshape(1, BLOCK)
    inner = 0.7978845608028654 * (value + 0.044715 * (value * value * value))
    value = 0.5 * value * (1.0 + jnp.tanh(inner))
    m.hidden[...] = value.astype(BF16).reshape(2, 256, BLOCK)

    sib_copies = {}

    def contract(offset):
        slot = OFFSETS.index(offset)
        at = lax.rem(z + offset + 8, 8)
        right = m.weights[at, 1].reshape(BLOCK, BLOCK)
        away = lax.dot_general(
            m.hidden[1 - k], right, (((1,), (1,)), ((), ())), preferred_element_type=F32
        )
        m.sib_out[slot] = away.astype(BF16)
        sib_copies[slot] = send(
            m.sib_out.at[slot],
            m.sib_in.at[slot],
            m.sib_send.at[slot],
            m.sib_recv.at[slot],
            sibling,
        )
        m.kept[slot] = lax.dot_general(
            m.hidden[k], right, (((1,), (1,)), ((), ())), preferred_element_type=F32
        )

    m_own = yh * 8 + s * 4 + x
    sum_copies = {}

    def scatter(g):
        first_slot = OFFSETS.index(GROUPS[g][0])
        count = len(GROUPS[g])
        for slot in range(first_slot, first_slot + count):
            sib_copies[slot].wait_recv()
            value = m.kept[slot] + m.sib_in[slot].astype(F32)
            m.outgoing[slot] = value.astype(BF16).reshape(16, 16, BLOCK)
        slots = pl.ds(first_slot, count)
        for dx in (2, 1, 3, 0):
            for dy in range(2):
                for ds in range(2):
                    if (dy, ds, dx) == (0, 0, 0):
                        continue
                    there = plane_place(dy, ds, dx)
                    m_there = lax.rem(yh + dy, 2) * 8 + there[0] * 4 + lax.rem(x + dx, 4)
                    index = dy * 8 + ds * 4 + dx
                    sum_copies[g, index] = send(
                        m.outgoing.at[slots, m_there],
                        m.incoming.at[slots, m_own],
                        m.sum_send.at[g, index],
                        m.sum_recv.at[g, index],
                        there,
                    )
        m.incoming[slots, m_own] = m.outgoing[slots, m_own]

    contract(0)
    arrive(1, 1)
    contract(-1)
    contract(1)
    scatter(0)
    ring_step(1, 3)
    arrive(1, 2)
    contract(-2)
    contract(2)
    scatter(1)
    ring_step(1, 4)
    arrive(1, 3)
    contract(-3)
    contract(3)
    scatter(2)
    arrive(1, 4)
    contract(4)
    scatter(3)

    for copy in base_copies:
        copy.wait_recv()
    row_sums = jnp.zeros((2, 8, 1), F32)
    row_squares = jnp.zeros((2, 8, 1), F32)
    for g in range(4):
        for index in range(1, 16):
            sum_copies[g, index].wait_recv()
        for offset in GROUPS[g]:
            slot = OFFSETS.index(offset)
            at = lax.rem(z + offset + 8, 8)
            branch = jnp.sum(m.incoming[slot].astype(F32), axis=0).reshape(2, 8, BLOCK)
            value = m.rows_in[at].reshape(2, 8, BLOCK) + m.final[0, at] * branch
            m.residual[slot] = value
            row_sums += jnp.sum(value, axis=2, keepdims=True)
            row_squares += jnp.sum(value * value, axis=2, keepdims=True)
    row_mean = row_sums * (1.0 / WIDTH)
    row_scale = lax.rsqrt(row_squares * (1.0 / WIDTH) - row_mean * row_mean + EPSILON)
    for copy in patch_copies:
        copy.wait_recv()
    projected = jnp.zeros((32, 128), F32)
    for slot in range(8):
        at = lax.rem(z + OFFSETS[slot] + 8, 8)
        value = (m.residual[slot] - row_mean) * row_scale * (1.0 + m.final[2, at]) + m.final[1, at]
        value = value.reshape(16, BLOCK)
        high = value.astype(BF16)
        low = (value - high.astype(F32)).astype(BF16)
        projected += jnp.dot(
            jnp.concatenate([high, low], axis=0), m.patch_all[at], preferred_element_type=F32
        )
    patch = projected[:16, :64] + (projected[16:, :64] + projected[:16, 64:])
    latent = (patch + patch_bias) / 0.3611 + 0.1159
    latent = jnp.concatenate([latent, jnp.zeros((16, 64), F32)], axis=1)
    m.latents[...] = latent
    m.blocks[1, 1, s] = latent

    copies = []
    for ds, dr, dc in halo:
        copy = pltpu.make_async_remote_copy(
            src_ref=m.latents,
            dst_ref=m.blocks.at[1 - dr, 1 - dc, s],
            send_sem=m.halo_send.at[ds, 1 - dr, 1 - dc],
            recv_sem=m.halo_recv.at[ds, 1 - dr, 1 - dc],
            device_id=place(ds, dr, dc),
            device_id_type=MESH,
        )
        copy.start()
        copies.append(copy)

    for copy in copies:
        copy.wait()

    for ds in range(2):
        for dr in (-1, 0, 1):
            for dc in (-1, 0, 1):
                inside = (r + dr >= 0) & (r + dr < N_ROW) & (c + dc >= 0) & (c + dc < N_COL)
                keep = jnp.where(inside, 1.0, 0.0).astype(jnp.float32)
                block = m.blocks[dr + 1, dc + 1, ds][:, :64] * keep
                rows = {-1: ((1, 0),), 0: ((0, 1), (1, 2)), 1: ((0, 3),)}[dr]
                first, count, at = {-1: (3, 1, 0), 0: (0, 4, 1), 1: (0, 1, 5)}[dc]
                for mb in range(2):
                    for source, target in rows:
                        start = mb * 8 + source * 4 + first
                        m.patches[2 * ds + mb, target, at : at + count, :] = block[
                            start : start + count
                        ]

    slabs = [
        m.patches[:, u : u + 3, v : v + 8, :].reshape(96, 64) for u in range(2) for v in range(2)
    ]
    window = jnp.concatenate(slabs, axis=-1)
    high = window.astype(jnp.bfloat16)
    low = (window - high.astype(jnp.float32)).astype(jnp.bfloat16)
    both = jnp.concatenate([high, low], axis=0)

    jj = lax.broadcasted_iota(jnp.int32, (96, 1), 0) % 8
    ii = (lax.broadcasted_iota(jnp.int32, (96, 1), 0) // 8) % 3
    sums = jnp.zeros((4, 512), jnp.float32)
    squares = jnp.zeros((4, 512), jnp.float32)
    for a in range(2):
        for b in range(2):
            phase = 2 * a + b
            lanes = pl.ds(phase * 512, 512)
            first = jnp.dot(both, m.taps[0, :, lanes], preferred_element_type=jnp.float32)
            second = jnp.dot(high, m.taps[1, :, lanes], preferred_element_type=jnp.float32)
            value = first[:96] + (first[96:] + second) + m.latent_bias[...]
            m.act[phase] = value
            own = (ii >= a) & (ii < a + 2) & (jj >= b) & (jj < b + 4)
            masked = jnp.where(own, value, 0.0).reshape(4, 24, 512)
            sums += jnp.sum(masked, axis=1)
            squares += jnp.sum(masked * masked, axis=1)

    chan = lax.broadcasted_iota(jnp.int32, (512, 128), 0) // 16
    member = (chan == lax.broadcasted_iota(jnp.int32, (512, 128), 1)).astype(jnp.float32)
    chan_t = lax.broadcasted_iota(jnp.int32, (128, 512), 1) // 16
    member_t = (chan_t == lax.broadcasted_iota(jnp.int32, (128, 512), 0)).astype(jnp.float32)
    stats = jnp.dot(
        jnp.concatenate([sums, squares], axis=0),
        member,
        preferred_element_type=jnp.float32,
        precision=lax.Precision.HIGHEST,
    )

    m.col_stats[c] = stats
    copies = []
    for dc in range(1, N_COL):
        copy = pltpu.make_async_remote_copy(
            src_ref=m.col_stats.at[c],
            dst_ref=m.col_stats.at[c],
            send_sem=m.col_send.at[dc],
            recv_sem=m.col_recv.at[dc],
            device_id=place(0, 0, dc),
            device_id_type=MESH,
        )
        copy.start()
        copies.append(copy)
    for copy in copies:
        copy.wait()
    m.row_stats[r] = jnp.sum(m.col_stats[...], axis=0)
    copies = []
    for dr in range(1, N_ROW):
        copy = pltpu.make_async_remote_copy(
            src_ref=m.row_stats.at[r],
            dst_ref=m.row_stats.at[r],
            send_sem=m.row_send.at[dr],
            recv_sem=m.row_recv.at[dr],
            device_id=place(0, dr, 0),
            device_id_type=MESH,
        )
        copy.start()
        copies.append(copy)
    for copy in copies:
        copy.wait()
    total = jnp.sum(m.row_stats[...], axis=0) * (1.0 / CELLS)
    mean = total[:4]
    scale = lax.rsqrt(total[4:] - mean * mean + EPSILON)
    spread = jnp.dot(
        jnp.concatenate([mean, scale], axis=0),
        member_t,
        preferred_element_type=jnp.float32,
        precision=lax.Precision.HIGHEST,
    )

    for a in range(2):
        for b in range(2):
            phase = 2 * a + b
            line = 4 * r + 2 * ii - a
            across = 8 * c + 2 * jj - b
            inside = (line >= 0) & (line < 64) & (across >= 0) & (across < 64)
            parts = []
            for mb in range(4):
                value = m.act[phase, mb * 24 : mb * 24 + 24]
                value = (value - spread[mb : mb + 1]) * (
                    spread[4 + mb : 5 + mb] * m.gain[...]
                ) + m.shift[...]
                parts.append(value / (1.0 + jnp.exp(-value)))
            value = jnp.where(inside, jnp.concatenate(parts, axis=0), 0.0)
            m.cells[phase * 96 : phase * 96 + 96, :] = value.astype(jnp.bfloat16)

    load_decode.wait()
    for tap in range(9):
        value = jnp.dot(m.cells[...], m.decode_in[tap], preferred_element_type=jnp.float32)
        m.products[tap] = value.reshape(4, 4, 3, 8, 256)

    for a in range(2):
        for b in range(2):
            for up in range(2):
                for left in range(2):
                    total = jnp.zeros((4, 2, 4, 256), jnp.float32) + m.decode_bias[...]
                    for di in range(3):
                        row_phase, row_at = phase_of(a, (up + di - 1) // 2)
                        for dj in range(3):
                            col_phase, col_at = phase_of(b, (left + dj - 1) // 2)
                            total += m.products[
                                di * 3 + dj,
                                row_phase * 2 + col_phase,
                                :,
                                row_at : row_at + 2,
                                col_at : col_at + 4,
                                :,
                            ]
                    for mb in range(4):
                        for i in range(2):
                            for half in range(2):
                                m.out[
                                    half,
                                    mb,
                                    4 * i + 2 * a + up,
                                    pl.ds(2 * b + left, 4, stride=4),
                                    :,
                                ] = total[mb, i, :, half * 128 : half * 128 + 128]

    for copy in from_partner:
        copy.wait_send()
    for copy in ring.values():
        copy.wait_send()
    for copy in sent:
        copy.wait_send()
    for copy in sib_copies.values():
        copy.wait_send()
    for copy in sum_copies.values():
        copy.wait_send()


def shards(*args):
    shapes = {
        "latent_bias": (1, 512),
        "gain": (1, 512),
        "shift": (1, 512),
        "decode_kernel": (9, 512, 256),
        "decode_bias": (1, 256),
    }
    turned = {"modulation": (1, 0, 2), "reduce": (1, 0), "patch": (1, 0)}
    args = [
        a.transpose(turned[name]) if name in turned else a.reshape(shapes.get(name, a.shape))
        for name, a in zip(INPUTS, args, strict=True)
    ]
    out = pl.pallas_call(
        program_kernel,
        out_shape=jax.ShapeDtypeStruct((2, 4, 8, 16, 128), F32),
        in_specs=[pl.BlockSpec(memory_space=space) for space in INPUTS.values()],
        out_specs=pl.BlockSpec(memory_space=pltpu.VMEM),
        scratch_shapes=list(SCRATCH.values()),
        compiler_params=pltpu.CompilerParams(
            collective_id=0, has_side_effects=True, vmem_limit_bytes=56 * 2**20
        ),
    )(*args)
    return out.transpose(1, 2, 3, 0, 4).reshape(4, 8, 16, 256)


def solution(mesh):
    return jax.shard_map(
        shards,
        mesh=mesh,
        in_specs=(
            P(None, "row", "col"),
            P(),
            P(),
            P("row", "col"),
            P("col"),
            P("col", "row"),
            P("col"),
            P("col", None),
            P(),
            P(),
            P(),
            P(),
            P(),
            P(None, None, None, "section"),
            P("section"),
        ),
        out_specs=P(None, "row", "col", "section"),
        check_vma=False,
    )
```

time: 575 us -> 99.1 us (0.17)
  waiting for transfers between devices: 376 us -> 0 us
  blocking collectives: 85 us -> 0 us
  Pallas kernels: 26 us -> 97 us
  matrix products: 54.1 us -> 0 us
  between operations: 21 us -> 0.01 us
  other arithmetic: 8.17 us -> 0 us
    all_gather x2 -> x0, waiting for transfers between devices: 254 us -> none  [the longest x1 146 us: shards(): lax.all_gather(reduce_weight, 'row', axis=1, tiled=True)]
    pallas_call x1, Pallas kernels: 26 us -> 97 us  [shards(): pl.pallas_call(program_kernel, out_shape=jax.ShapeDtypeStruct((2, 4, 8, 1...]
    psum x1 -> x0, waiting for transfers between devices: 62 us -> none  [shards(): patches = lax.psum(local_proj, 'col')]
    reduce_scatter x4 -> x0, waiting for transfers between devices: 58.6 us -> none  [shards(): lax.psum_scatter(partial_branch, 'col', scatter_dimension=1, tiled=True)]
    all_gather x4 -> x0, blocking collectives: 55 us -> none  [shards(): tower_normed_all = lax.all_gather(normed, 'col', axis=1, tiled=True)]
    dot_general x8 -> x0, matrix products: 54.1 us -> none  [the longest x4 47.7 us: run_branch(): return jnp.dot(hidden, reduce_full, preferred_element_type=jnp.float32)]
    psum x2 -> x0, blocking collectives: 30 us -> none  [the longest x1 15 us: shards(): lax.psum((jnp.sum(rows_in, axis=1), jnp.sum(rows_in * rows_in, axis=1)),...]
  transfers between devices with their start and end apart: 7 -> 0, of which waited for: 5 -> 0; matrix products, arithmetic and copies ran while one was open for 7% -> 0% of each run, Pallas kernels for 0% -> 0%
where the time goes in v3:
time: 99.1 us; the launch traced here: 98.9 us
  Pallas kernels  97 us (98%)
  local copies, waits for them, and re-layouts  1.9 us (2%)
    pallas_call x1, Pallas kernels, shards(): pl.pallas_call(program_kernel, out_shape=jax.ShapeDtypeStruct((2, 4, 8, 1...  97 us

profile of v3, /device:TPU:1, one launch (start us, length us, event | category | flops | bytes accessed | tf_op | source)
XLA Modules:
  0.0 98.9 jit_solution(16179144268174936714)
XLA Ops:
  0.0 97.0 %shard_map.145 = f32[2,4,8,16,128]{4,3,2,1,0:T(8,128)} custom-call(f32[4,64,384]{2,1,0:T(8,128)} %refs_0_.1, s32[4]{0:T(128)} %refs_1_.1, f32[5,4,3072]{2,1,0:T(4,128)} %bitcast.16, bf16[192,1536]{1,0:T(8,128)(2,1)} %refs_3_.1, f32[1536]{0:T(1024)} %refs_4_.1, bf16[192,1536]{1,0:T(8,128)(2,1)} %bitcast.15, f32[384]{0:T(512)} %refs_6_.1, f32[64,384]{1,0:T(8,128)} %bitcast.17, ...), custom_call_target="tpu_custom_call" | custom-call | tf_op jit(solution)/shard_map/pallas_call | solution.py:696
  97.0 1.9 %copy_bitcast_fusion = f32[4,8,16,256]{3,2,1,0:T(8,128)} fusion(f32[2,4,8,16,128]{4,3,2,1,0:T(8,128)} %shard_map.145), kind=kLoop, calls=%fused_computation | loop fusion | bytes 1048576 | tf_op jit(solution)/shard_map/reshape | solution.py:706

commit v4 on v3

--- a/solution.py
+++ b/solution.py
@@ -67,6 +67,9 @@
     "products": pltpu.VMEM((9, 4, 4, 3, 8, 256), F32),
     "col_stats": pltpu.VMEM((8, 8, 128), F32),
     "row_stats": pltpu.VMEM((16, 8, 128), F32),
+    "staged": pltpu.VMEM((2, 4, 8, 16, 128), F32),
+    "member": pltpu.VMEM((512, 128), F32),
+    "member_t": pltpu.VMEM((128, 512), F32),
     "load_sem": DMA((8,)),
     "partner_send": DMA((2,)),
     "partner_recv": DMA((2,)),
@@ -76,8 +79,8 @@
     "stat_recv": DMA((8,)),
     "base_send": DMA((8,)),
     "base_recv": DMA((8,)),
-    "patch_send": DMA((8,)),
-    "patch_recv": DMA((8,)),
+    "patch_send": DMA((2, 4)),
+    "patch_recv": DMA((2, 4)),
     "tok_send": DMA((2, 4)),
     "tok_recv": DMA((2, 4)),
     "fwd_send": DMA((2, 4)),
@@ -248,69 +251,6 @@
     for slot in range(4):
         for j in range(3):
             m.first[j, slot // 2, slot % 2] = m.factors[j, pl.ds(m.order[slot], 1), lanes]
-
-    for copy in stat_copies:
-        copy.wait_recv()
-    table = jnp.concatenate([jnp.sum(m.stats[...], axis=0), jnp.zeros((120, 256), F32)], axis=0).T
-    token_mean = table[:, 0:1] * (1.0 / WIDTH)
-    token_scale = lax.rsqrt(table[:, 1:2] * (1.0 / WIDTH) - token_mean * token_mean + EPSILON)
-    plain = (tok - token_mean) * token_scale
-    for core in range(2):
-        for group in range(8):
-            start = core * 128 + group * 16
-            part = plain[start : start + 16].reshape(2, 8, BLOCK)
-            part = part * (1.0 + m.first[1, group // 4]) + m.first[0, group // 4]
-            m.normed[c, core, yh, pl.ds(group * 16, 16), :] = part.reshape(16, BLOCK).astype(BF16)
-
-    mine = m.normed.at[c, :, yh]
-    tok_copies = {}
-    for dy, dx in ((1, 0), (0, 1), (0, 3), (1, 1), (1, 3), (0, 2), (1, 2)):
-        tok_copies[dy, dx] = send(
-            mine, mine, m.tok_send.at[dy, dx], m.tok_recv.at[dy, dx], plane_place(dy, dy, dx)
-        )
-    tok_copies[0, 0] = send(mine, mine, m.tok_send.at[0, 0], m.tok_recv.at[0, 0], sibling)
-    sent += tok_copies.values()
-
-    ring_step(0, 2)
-
-    for copy in load_reduce:
-        copy.wait()
-    from_partner.append(to_partner(1, m.reduce.at[:, other_cols]))
-
-    for core in range(2):
-        for group in range(8):
-            rows = pl.ds(group * 16, 16)
-            part = m.tok[core, rows, :].reshape(2, 8, BLOCK)
-            part = part + m.first[2, group // 4] * m.reduce_bias[...].reshape(1, BLOCK)
-            m.based[core, rows, :] = part.reshape(16, BLOCK)
-    base_copies = []
-    for d in range(1, 8):
-        target = lax.rem(c + d, 8)
-        rows = pl.ds(pl.multiple_of((s * 4 + target // 2) * 16, 16), 16)
-        base_copies.append(
-            send(
-                m.based.at[target % 2, rows, :],
-                m.rows_in.at[c],
-                m.base_send.at[d],
-                m.base_recv.at[d],
-                col_place(d),
-            )
-        )
-    sent += base_copies
-    own_rows = pl.ds(pl.multiple_of((s * 4 + x) * 16, 16), 16)
-    m.rows_in[c] = m.based[k, own_rows, :]
-
-    forwards = []
-
-    def forward(dy, dx):
-        tok_copies[dy, dx].wait_recv()
-        piece = m.normed.at[2 * lax.rem(x - dx + 4, 4) + k, :, lax.rem(yh + dy, 2)]
-        forwards.append(send(piece, piece, m.fwd_send.at[dy, dx], m.fwd_recv.at[dy, dx], sibling))
-
-    forward(1, 0)
-    ring_step(0, 3)
-    for dy, dx in ((0, 1), (0, 3)):
-        forward(dy, dx)
 
     source = lax.broadcasted_iota(jnp.int32, (64, 64), 0)
     target = lax.broadcasted_iota(jnp.int32, (64, 64), 1)
@@ -349,6 +289,10 @@
                                 m.taps[0, rows, lanes] = high
                                 m.taps[1, rows, lanes] = low
     m.patches[...] = jnp.zeros_like(m.patches)
+    chan = lax.broadcasted_iota(jnp.int32, (512, 128), 0) // 16
+    m.member[...] = (chan == lax.broadcasted_iota(jnp.int32, (512, 128), 1)).astype(jnp.float32)
+    chan_t = lax.broadcasted_iota(jnp.int32, (128, 512), 1) // 16
+    m.member_t[...] = (chan_t == lax.broadcasted_iota(jnp.int32, (128, 512), 0)).astype(jnp.float32)
 
     for slot in range(2):
         for j in range(3):
@@ -357,25 +301,95 @@
                     j + 2, pl.ds(m.order[2 * s + slot], 1), at * BLOCK : (at + 1) * BLOCK
                 ]
 
-    ring_step(1, 1, (0,))
-    for dy, dx in ((1, 1), (1, 3)):
+    for copy in stat_copies:
+        copy.wait_recv()
+    ring_step(0, 2, (0,))
+    table = jnp.concatenate([jnp.sum(m.stats[...], axis=0), jnp.zeros((120, 256), F32)], axis=0).T
+    token_mean = table[:, 0:1] * (1.0 / WIDTH)
+    token_scale = lax.rsqrt(table[:, 1:2] * (1.0 / WIDTH) - token_mean * token_mean + EPSILON)
+    plain = (tok - token_mean) * token_scale
+    for core in range(2):
+        for group in range(8):
+            start = core * 128 + group * 16
+            part = plain[start : start + 16].reshape(2, 8, BLOCK)
+            part = part * (1.0 + m.first[1, group // 4]) + m.first[0, group // 4]
+            m.normed[c, core, yh, pl.ds(group * 16, 16), :] = part.reshape(16, BLOCK).astype(BF16)
+
+    tok_copies = {}
+
+    def share(dy, dx, col, half, target):
+        piece = m.normed.at[col, :, half]
+        tok_copies[dy, dx] = send(
+            piece, piece, m.tok_send.at[dy, dx], m.tok_recv.at[dy, dx], target
+        )
+
+    share(1, 0, c, yh, partner)
+    for dx in (3, 1, 2):
+        share(0, dx, c, yh, plane_place(0, 0, dx))
+    share(0, 0, c, yh, sibling)
+
+    ring_step(0, 2, (1,))
+
+    for copy in load_reduce:
+        copy.wait()
+    from_partner.append(to_partner(1, m.reduce.at[:, other_cols]))
+
+    for core in range(2):
+        for group in range(8):
+            rows = pl.ds(group * 16, 16)
+            part = m.tok[core, rows, :].reshape(2, 8, BLOCK)
+            part = part + m.first[2, group // 4] * m.reduce_bias[...].reshape(1, BLOCK)
+            m.based[core, rows, :] = part.reshape(16, BLOCK)
+    base_copies = []
+    for d in range(1, 8):
+        target = lax.rem(c + d, 8)
+        rows = pl.ds(pl.multiple_of((s * 4 + target // 2) * 16, 16), 16)
+        base_copies.append(
+            send(
+                m.based.at[target % 2, rows, :],
+                m.rows_in.at[c],
+                m.base_send.at[d],
+                m.base_recv.at[d],
+                col_place(d),
+            )
+        )
+    sent += base_copies
+    own_rows = pl.ds(pl.multiple_of((s * 4 + x) * 16, 16), 16)
+    m.rows_in[c] = m.based[k, own_rows, :]
+
+    forwards = []
+
+    def forward(dy, dx):
+        tok_copies[dy, dx].wait_recv()
+        col, half = 2 * lax.rem(x - dx + 4, 4) + k, lax.rem(yh + dy, 2)
+        if (dy, dx) == (1, 0):
+            share(1, 1, col, half, plane_place(0, 0, 1))
+        if dy == 0 and dx > 1:
+            share(1, dx, col, half, partner)
+        piece = m.normed.at[col, :, half]
+        forwards.append(send(piece, piece, m.fwd_send.at[dy, dx], m.fwd_recv.at[dy, dx], sibling))
+
+    for dy, dx in ((1, 0), (0, 3), (0, 1)):
+        forward(dy, dx)
+    ring_step(0, 3)
+    for dy, dx in ((0, 2), (1, 1), (1, 3)):
         forward(dy, dx)
     ring_step(0, 4)
     from_partner[1].wait_recv()
-    ring_step(1, 1, (1,))
-    for dy, dx in ((0, 2), (1, 2)):
-        forward(dy, dx)
+    ring_step(1, 1)
+    forward(1, 2)
     sent += forwards
+    sent += tok_copies.values()
 
     patch_copies = [
         send(
             m.patch_all.at[c],
             m.patch_all.at[c],
-            m.patch_send.at[d],
-            m.patch_recv.at[d],
-            col_place(d),
-        )
-        for d in range(1, 8)
+            m.patch_send.at[0, d],
+            m.patch_recv.at[0, d],
+            plane_place(0, 0, d) if d else sibling,
+        )
+        for d in (1, 3, 2, 0)
     ]
     sent += patch_copies
 
@@ -398,7 +412,6 @@
     arrive(0, 2)
     for offset in OFFSETS[:5]:
         expand(offset)
-    ring_step(1, 2)
     arrive(0, 3)
     expand(-3)
     expand(3)
@@ -458,7 +471,35 @@
                     )
         m.incoming[slots, m_own] = m.outgoing[slots, m_own]
 
+    row_parts = []
+
+    def collect(g):
+        for index in range(1, 16):
+            sum_copies[g, index].wait_recv()
+        for offset in GROUPS[g]:
+            slot = OFFSETS.index(offset)
+            at = lax.rem(z + offset + 8, 8)
+            branch = jnp.sum(m.incoming[slot].astype(F32), axis=0).reshape(2, 8, BLOCK)
+            value = m.rows_in[at].reshape(2, 8, BLOCK) + m.final[0, at] * branch
+            m.residual[slot] = value
+            row_parts.append(
+                (
+                    jnp.sum(value, axis=2, keepdims=True),
+                    jnp.sum(value * value, axis=2, keepdims=True),
+                )
+            )
+
+    patch_forwards = []
+    for d, copy in zip((1, 3, 2), patch_copies):
+        copy.wait_recv()
+        piece = m.patch_all.at[2 * lax.rem(x - d + 4, 4) + k]
+        patch_forwards.append(
+            send(piece, piece, m.patch_send.at[1, d], m.patch_recv.at[1, d], sibling)
+        )
+    sent += patch_forwards
+
     contract(0)
+    ring_step(1, 2)
     arrive(1, 1)
     contract(-1)
     contract(1)
@@ -469,32 +510,23 @@
     contract(2)
     scatter(1)
     ring_step(1, 4)
+    for copy in base_copies:
+        copy.wait_recv()
     arrive(1, 3)
     contract(-3)
     contract(3)
     scatter(2)
+    collect(0)
     arrive(1, 4)
     contract(4)
     scatter(3)
-
-    for copy in base_copies:
-        copy.wait_recv()
-    row_sums = jnp.zeros((2, 8, 1), F32)
-    row_squares = jnp.zeros((2, 8, 1), F32)
-    for g in range(4):
-        for index in range(1, 16):
-            sum_copies[g, index].wait_recv()
-        for offset in GROUPS[g]:
-            slot = OFFSETS.index(offset)
-            at = lax.rem(z + offset + 8, 8)
-            branch = jnp.sum(m.incoming[slot].astype(F32), axis=0).reshape(2, 8, BLOCK)
-            value = m.rows_in[at].reshape(2, 8, BLOCK) + m.final[0, at] * branch
-            m.residual[slot] = value
-            row_sums += jnp.sum(value, axis=2, keepdims=True)
-            row_squares += jnp.sum(value * value, axis=2, keepdims=True)
+    for g in range(1, 4):
+        collect(g)
+    row_sums = sum(part[0] for part in row_parts)
+    row_squares = sum(part[1] for part in row_parts)
     row_mean = row_sums * (1.0 / WIDTH)
     row_scale = lax.rsqrt(row_squares * (1.0 / WIDTH) - row_mean * row_mean + EPSILON)
-    for copy in patch_copies:
+    for copy in (patch_copies[3], *patch_forwards):
         copy.wait_recv()
     projected = jnp.zeros((32, 128), F32)
     for slot in range(8):
@@ -526,7 +558,8 @@
         copies.append(copy)
 
     for copy in copies:
-        copy.wait()
+        copy.wait_recv()
+    sent += copies
 
     for ds in range(2):
         for dr in (-1, 0, 1):
@@ -568,13 +601,9 @@
             sums += jnp.sum(masked, axis=1)
             squares += jnp.sum(masked * masked, axis=1)
 
-    chan = lax.broadcasted_iota(jnp.int32, (512, 128), 0) // 16
-    member = (chan == lax.broadcasted_iota(jnp.int32, (512, 128), 1)).astype(jnp.float32)
-    chan_t = lax.broadcasted_iota(jnp.int32, (128, 512), 1) // 16
-    member_t = (chan_t == lax.broadcasted_iota(jnp.int32, (128, 512), 0)).astype(jnp.float32)
     stats = jnp.dot(
         jnp.concatenate([sums, squares], axis=0),
-        member,
+        m.member[...],
         preferred_element_type=jnp.float32,
         precision=lax.Precision.HIGHEST,
     )
@@ -593,7 +622,8 @@
         copy.start()
         copies.append(copy)
     for copy in copies:
-        copy.wait()
+        copy.wait_recv()
+    sent += copies
     m.row_stats[r] = jnp.sum(m.col_stats[...], axis=0)
     copies = []
     for dr in range(1, N_ROW):
@@ -608,13 +638,14 @@
         copy.start()
         copies.append(copy)
     for copy in copies:
-        copy.wait()
+        copy.wait_recv()
+    sent += copies
     total = jnp.sum(m.row_stats[...], axis=0) * (1.0 / CELLS)
     mean = total[:4]
     scale = lax.rsqrt(total[4:] - mean * mean + EPSILON)
     spread = jnp.dot(
         jnp.concatenate([mean, scale], axis=0),
-        member_t,
+        m.member_t[...],
         preferred_element_type=jnp.float32,
         precision=lax.Precision.HIGHEST,
     )
@@ -660,13 +691,19 @@
                     for mb in range(4):
                         for i in range(2):
                             for half in range(2):
-                                m.out[
+                                m.staged[
                                     half,
                                     mb,
                                     4 * i + 2 * a + up,
                                     pl.ds(2 * b + left, 4, stride=4),
                                     :,
                                 ] = total[mb, i, :, half * 128 : half * 128 + 128]
+    stores = [
+        load(m.staged.at[half], m.out.at[:, :, :, pl.ds(half * 128, 128)], half)
+        for half in range(2)
+    ]
+    for copy in stores:
+        copy.wait()
 
     for copy in from_partner:
         copy.wait_send()
@@ -693,17 +730,16 @@
         a.transpose(turned[name]) if name in turned else a.reshape(shapes.get(name, a.shape))
         for name, a in zip(INPUTS, args, strict=True)
     ]
-    out = pl.pallas_call(
+    return pl.pallas_call(
         program_kernel,
-        out_shape=jax.ShapeDtypeStruct((2, 4, 8, 16, 128), F32),
+        out_shape=jax.ShapeDtypeStruct((4, 8, 16, 256), F32),
         in_specs=[pl.BlockSpec(memory_space=space) for space in INPUTS.values()],
-        out_specs=pl.BlockSpec(memory_space=pltpu.VMEM),
+        out_specs=pl.BlockSpec(memory_space=pl.ANY),
         scratch_shapes=list(SCRATCH.values()),
         compiler_params=pltpu.CompilerParams(
             collective_id=0, has_side_effects=True, vmem_limit_bytes=56 * 2**20
         ),
     )(*args)
-    return out.transpose(1, 2, 3, 0, 4).reshape(4, 8, 16, 256)
 
 
 def solution(mesh):

time: 99.1 us -> 93.5 us (0.943)
  Pallas kernels: 97 us -> 91.4 us
    pallas_call x1, Pallas kernels: 97 us -> 91.4 us  [shards(): pl.pallas_call(program_kernel, out_shape=jax.ShapeDtypeStruct((4, 8, 16,...]
    reshape x1 -> x0, local copies, waits for them, and re-layouts: 1.9 us -> none  [shards(): return out.transpose(1, 2, 3, 0, 4).reshape(4, 8, 16, 256)]
    unnamed x0 -> x1, local copies, waits for them, and re-layouts: none -> 1.87 us
where the time goes in v4:
time: 93.5 us; the launch traced here: 93.3 us
  Pallas kernels  91.4 us (98%)
  local copies, waits for them, and re-layouts  1.87 us (2%)
    pallas_call x1, Pallas kernels, shards(): pl.pallas_call(program_kernel, out_shape=jax.ShapeDtypeStruct((4, 8, 16,...  91.4 us

profile of v4, /device:TPU:1, one launch (start us, length us, event | category | flops | bytes accessed | tf_op | source)
XLA Modules:
  0.0 93.3 jit_solution(13600710779583280846)
XLA Ops:
  0.0 91.4 %shard_map.145 = f32[4,8,16,256]{3,2,1,0:T(8,128)} custom-call(f32[4,64,384]{2,1,0:T(8,128)} %refs_0_.1, s32[4]{0:T(128)} %refs_1_.1, f32[5,4,3072]{2,1,0:T(4,128)} %bitcast.10, bf16[192,1536]{1,0:T(8,128)(2,1)} %refs_3_.1, f32[1536]{0:T(1024)} %refs_4_.1, bf16[192,1536]{1,0:T(8,128)(2,1)} %bitcast.9, f32[384]{0:T(512)} %refs_6_.1, f32[64,384]{1,0:T(8,128)} %bitcast.11, ...), custom_call_target="tpu_custom_call" | custom-call | tf_op jit(solution)/shard_map/pallas_call | solution.py:733
  91.4 1.9 %copy.17 = f32[4,8,16,256]{3,2,1,0:T(8,128)} copy(f32[4,8,16,256]{3,2,1,0:T(8,128)} %shard_map.145) | data formatting | bytes 1048576

commit v5 on v4

--- a/solution.py
+++ b/solution.py
@@ -56,6 +56,8 @@
     "sib_in": pltpu.VMEM((8, 256, BLOCK), BF16),
     "kept": pltpu.VMEM((8, 256, BLOCK), F32),
     "outgoing": pltpu.VMEM((8, 16, 16, BLOCK), BF16),
+    "middle": pltpu.VMEM((7, 4, 4, 16, BLOCK), BF16),
+    "second": pltpu.VMEM((7, 4, 16, BLOCK), BF16),
     "incoming": pltpu.VMEM((8, 16, 16, BLOCK), BF16),
     "residual": pltpu.VMEM((8, 2, 8, BLOCK), F32),
     "latents": pltpu.VMEM((16, 128), F32),
@@ -68,8 +70,8 @@
     "col_stats": pltpu.VMEM((8, 8, 128), F32),
     "row_stats": pltpu.VMEM((16, 8, 128), F32),
     "staged": pltpu.VMEM((2, 4, 8, 16, 128), F32),
-    "member": pltpu.VMEM((512, 128), F32),
-    "member_t": pltpu.VMEM((128, 512), F32),
+    "member": pltpu.VMEM((512, 128), BF16),
+    "member_t": pltpu.VMEM((128, 512), BF16),
     "load_sem": DMA((8,)),
     "partner_send": DMA((2,)),
     "partner_recv": DMA((2,)),
@@ -104,6 +106,19 @@
     return [(0, 0), (1, 1), (0, 1)][step + 1]
 
 
+def thirds(value):
+    parts = []
+    for _ in range(3):
+        parts.append(value.astype(BF16))
+        value = value - parts[-1].astype(F32)
+    return jnp.concatenate(parts, axis=0)
+
+
+def gathered(value, member):
+    product = jnp.dot(thirds(value), member, preferred_element_type=F32)
+    return product[:8] + (product[8:16] + product[16:])
+
+
 def program_kernel(*refs):
     names = [*INPUTS, "out", *SCRATCH]
     m = SimpleNamespace(**dict(zip(names, refs, strict=True)))
@@ -146,6 +161,22 @@
             lax.rem(c + dc + N_COL, N_COL),
         )
 
+    halo = []
+    for ds in range(2):
+        for dr in (-1, 0, 1):
+            for dc in (-1, 0, 1):
+                if (ds, dr, dc) != (0, 0, 0):
+                    halo.append((ds, dr, dc))
+
+    barrier = pltpu.get_barrier_semaphore()
+    greet = [place(0, step, 0) for step in range(1, N_ROW)]
+    greet += [col_place(step) for step in range(1, N_COL)]
+    for dy, ds in ((0, 1), (1, 0), (1, 1)):
+        greet += [plane_place(dy, ds, dx) for dx in range(4)]
+    greet += [place(*h) for h in halo if h[0] * (h[1] or h[2]) or h[1] * h[2]]
+    for target in greet:
+        pl.semaphore_signal(barrier, inc=1, device_id=target, device_id_type=MESH)
+
     def load(source, target, index):
         copy = pltpu.make_async_copy(source, target, m.load_sem.at[index])
         copy.start()
@@ -162,21 +193,6 @@
     load_latent = load(m.latent_kernel, m.latent_in, 5)
     load_decode = load(m.decode_kernel, m.decode_in, 6)
 
-    halo = []
-    for ds in range(2):
-        for dr in (-1, 0, 1):
-            for dc in (-1, 0, 1):
-                if (ds, dr, dc) != (0, 0, 0):
-                    halo.append((ds, dr, dc))
-
-    barrier = pltpu.get_barrier_semaphore()
-    greet = [place(0, step, 0) for step in range(1, N_ROW)]
-    greet += [col_place(step) for step in range(1, N_COL)]
-    for dy, ds in ((0, 1), (1, 0), (1, 1)):
-        greet += [plane_place(dy, ds, dx) for dx in range(4)]
-    greet += [place(*h) for h in halo if h[0] * (h[1] or h[2]) or h[1] * h[2]]
-    for target in greet:
-        pl.semaphore_signal(barrier, inc=1, device_id=target, device_id_type=MESH)
     pl.semaphore_wait(barrier, len(greet))
 
     def to_partner(e, source):
@@ -184,7 +200,6 @@
             source, m.weights.at[z, e, yh], m.partner_send.at[e], m.partner_recv.at[e], partner
         )
 
-    from_partner = [to_partner(0, m.expand.at[:, other_cols])]
     ring = {}
     arrived = set()
 
@@ -222,6 +237,7 @@
 
     load_expand.wait()
     ring_step(0, 1, (0,))
+    from_partner = [to_partner(0, m.expand.at[:, other_cols])]
 
     load_tokens.wait()
     for slot in range(4):
@@ -290,9 +306,9 @@
                                 m.taps[1, rows, lanes] = low
     m.patches[...] = jnp.zeros_like(m.patches)
     chan = lax.broadcasted_iota(jnp.int32, (512, 128), 0) // 16
-    m.member[...] = (chan == lax.broadcasted_iota(jnp.int32, (512, 128), 1)).astype(jnp.float32)
+    m.member[...] = (chan == lax.broadcasted_iota(jnp.int32, (512, 128), 1)).astype(F32).astype(BF16)
     chan_t = lax.broadcasted_iota(jnp.int32, (128, 512), 1) // 16
-    m.member_t[...] = (chan_t == lax.broadcasted_iota(jnp.int32, (128, 512), 0)).astype(jnp.float32)
+    m.member_t[...] = (chan_t == lax.broadcasted_iota(jnp.int32, (128, 512), 0)).astype(F32).astype(BF16)
 
     for slot in range(2):
         for j in range(3):
@@ -489,6 +505,12 @@
                 )
             )
 
+    contract(0)
+    ring_step(1, 2)
+    arrive(1, 1)
+    contract(-1)
+    contract(1)
+    scatter(0)
     patch_forwards = []
     for d, copy in zip((1, 3, 2), patch_copies):
         copy.wait_recv()
@@ -497,13 +519,6 @@
             send(piece, piece, m.patch_send.at[1, d], m.patch_recv.at[1, d], sibling)
         )
     sent += patch_forwards
-
-    contract(0)
-    ring_step(1, 2)
-    arrive(1, 1)
-    contract(-1)
-    contract(1)
-    scatter(0)
     ring_step(1, 3)
     arrive(1, 2)
     contract(-2)
@@ -601,12 +616,7 @@
             sums += jnp.sum(masked, axis=1)
             squares += jnp.sum(masked * masked, axis=1)
 
-    stats = jnp.dot(
-        jnp.concatenate([sums, squares], axis=0),
-        m.member[...],
-        preferred_element_type=jnp.float32,
-        precision=lax.Precision.HIGHEST,
-    )
+    stats = gathered(jnp.concatenate([sums, squares], axis=0), m.member[...])
 
     m.col_stats[c] = stats
     copies = []
@@ -643,12 +653,7 @@
     total = jnp.sum(m.row_stats[...], axis=0) * (1.0 / CELLS)
     mean = total[:4]
     scale = lax.rsqrt(total[4:] - mean * mean + EPSILON)
-    spread = jnp.dot(
-        jnp.concatenate([mean, scale], axis=0),
-        m.member_t[...],
-        preferred_element_type=jnp.float32,
-        precision=lax.Precision.HIGHEST,
-    )
+    spread = gathered(jnp.concatenate([mean, scale], axis=0), m.member_t[...])
 
     for a in range(2):
         for b in range(2):

time: 93.5 us -> 93.3 us (level)
  no operation moved by 1% of the time
where the time goes in v5:
time: 93.3 us; the launch traced here: 93.2 us
  Pallas kernels  91.3 us (98%)
  local copies, waits for them, and re-layouts  1.87 us (2%)
    pallas_call x1, Pallas kernels, shards(): pl.pallas_call(program_kernel, out_shape=jax.ShapeDtypeStruct((4, 8, 16,...  91.3 us
    unnamed x1, local copies, waits for them, and re-layouts  1.87 us

profile of v5, /device:TPU:1, one launch (start us, length us, event | category | flops | bytes accessed | tf_op | source)
XLA Modules:
  0.0 93.2 jit_solution(3952264336381178673)
XLA Ops:
  0.0 91.3 %shard_map.145 = f32[4,8,16,256]{3,2,1,0:T(8,128)} custom-call(f32[4,64,384]{2,1,0:T(8,128)} %refs_0_.1, s32[4]{0:T(128)} %refs_1_.1, f32[5,4,3072]{2,1,0:T(4,128)} %bitcast.10, bf16[192,1536]{1,0:T(8,128)(2,1)} %refs_3_.1, f32[1536]{0:T(1024)} %refs_4_.1, bf16[192,1536]{1,0:T(8,128)(2,1)} %bitcast.9, f32[384]{0:T(512)} %refs_6_.1, f32[64,384]{1,0:T(8,128)} %bitcast.11, ...), custom_call_target="tpu_custom_call" | custom-call | tf_op jit(solution)/shard_map/pallas_call | solution.py:738
  91.3 1.9 %copy.17 = f32[4,8,16,256]{3,2,1,0:T(8,128)} copy(f32[4,8,16,256]{3,2,1,0:T(8,128)} %shard_map.145) | data formatting | bytes 1048576

commit v6 on v5

--- a/solution.py
+++ b/solution.py
@@ -20,21 +20,31 @@
 BF16, F32 = jnp.bfloat16, jnp.float32
 DMA = pltpu.SemaphoreType.DMA
 INPUTS = {
-    "tokens": pl.ANY,
+    "tokens": pltpu.HBM,
     "order": pltpu.SMEM,
-    "modulation": pl.ANY,
-    "expand": pl.ANY,
-    "expand_bias": pltpu.VMEM,
-    "reduce": pl.ANY,
-    "reduce_bias": pltpu.VMEM,
-    "patch": pltpu.VMEM,
-    "patch_bias": pltpu.VMEM,
-    "latent_kernel": pl.ANY,
-    "latent_bias": pltpu.VMEM,
-    "gain": pltpu.VMEM,
-    "shift": pltpu.VMEM,
-    "decode_kernel": pl.ANY,
-    "decode_bias": pltpu.VMEM,
+    "modulation": pltpu.HBM,
+    "expand": pltpu.HBM,
+    "expand_bias": pltpu.HBM,
+    "reduce": pltpu.HBM,
+    "reduce_bias": pltpu.HBM,
+    "patch": pltpu.HBM,
+    "patch_bias": pltpu.HBM,
+    "latent_kernel": pltpu.HBM,
+    "latent_bias": pltpu.HBM,
+    "gain": pltpu.HBM,
+    "shift": pltpu.HBM,
+    "decode_kernel": pltpu.HBM,
+    "decode_bias": pltpu.HBM,
+}
+SMALL = {
+    "expand_bias": (1536,),
+    "reduce_bias": (BLOCK,),
+    "patch": (64, BLOCK),
+    "patch_bias": (64,),
+    "latent_bias": (1, 512),
+    "gain": (1, 512),
+    "shift": (1, 512),
+    "decode_bias": (1, 256),
 }
 SCRATCH = {
     "tokens_in": pltpu.VMEM((4, 64, BLOCK), F32),
@@ -72,7 +82,8 @@
     "staged": pltpu.VMEM((2, 4, 8, 16, 128), F32),
     "member": pltpu.VMEM((512, 128), BF16),
     "member_t": pltpu.VMEM((128, 512), BF16),
-    "load_sem": DMA((8,)),
+    **{name + "_in": pltpu.VMEM(shape, F32) for name, shape in SMALL.items()},
+    "load_sem": DMA((16,)),
     "partner_send": DMA((2,)),
     "partner_recv": DMA((2,)),
     "ring_send": DMA((2, 2, 2, 4)),
@@ -191,6 +202,11 @@
         load(m.reduce.at[:, own_cols], m.weights.at[z, 1, yh], 3),
     ]
     load_latent = load(m.latent_kernel, m.latent_in, 5)
+    small = []
+    for index, name in enumerate(SMALL):
+        held = getattr(m, name + "_in")
+        small.append(load(getattr(m, name), held, 8 + index))
+        setattr(m, name, held)
     load_decode = load(m.decode_kernel, m.decode_in, 6)
 
     pl.semaphore_wait(barrier, len(greet))
@@ -237,6 +253,8 @@
 
     load_expand.wait()
     ring_step(0, 1, (0,))
+    for copy in small:
+        copy.wait()
     from_partner = [to_partner(0, m.expand.at[:, other_cols])]
 
     load_tokens.wait()
@@ -742,7 +760,7 @@
         out_specs=pl.BlockSpec(memory_space=pl.ANY),
         scratch_shapes=list(SCRATCH.values()),
         compiler_params=pltpu.CompilerParams(
-            collective_id=0, has_side_effects=True, vmem_limit_bytes=56 * 2**20
+            collective_id=0, has_side_effects=True, vmem_limit_bytes=58 * 2**20
         ),
     )(*args)
 

time: 93.3 us -> 93.2 us (level)
  no operation moved by 1% of the time
where the time goes in v6:
time: 93.2 us; the launch traced here: 93 us
  Pallas kernels  91.2 us (98%)
  local copies, waits for them, and re-layouts  1.87 us (2%)
    pallas_call x1, Pallas kernels, shards(): pl.pallas_call(program_kernel, out_shape=jax.ShapeDtypeStruct((4, 8, 16,...  91.2 us
    unnamed x1, local copies, waits for them, and re-layouts  1.87 us

profile of v6, /device:TPU:1, one launch (start us, length us, event | category | flops | bytes accessed | tf_op | source)
XLA Modules:
  0.0 93.0 jit_solution(5338774233655170992)
XLA Ops:
  0.0 91.2 %shard_map.145 = f32[4,8,16,256]{3,2,1,0:T(8,128)} custom-call(f32[4,64,384]{2,1,0:T(8,128)} %refs_0_.1, s32[4]{0:T(128)} %refs_1_.1, f32[5,4,3072]{2,1,0:T(4,128)} %bitcast.10, bf16[192,1536]{1,0:T(8,128)(2,1)} %refs_3_.1, f32[1536]{0:T(1024)} %refs_4_.1, bf16[192,1536]{1,0:T(8,128)(2,1)} %bitcast.9, f32[384]{0:T(512)} %refs_6_.1, f32[64,384]{1,0:T(8,128)} %bitcast.11, ...), custom_call_target="tpu_custom_call" | custom-call | tf_op jit(solution)/shard_map/pallas_call | solution.py:756
  91.2 1.9 %copy.17 = f32[4,8,16,256]{3,2,1,0:T(8,128)} copy(f32[4,8,16,256]{3,2,1,0:T(8,128)} %shard_map.145) | data formatting | bytes 1048576
